TPU v7x, 512 devices: a whole 4x8x8 slice. The times are simulated.
512 devices in a mesh: band: 32 (over x, z), grid: 16 (over y, core).
Axes of the slice: x: 4, y: 8, z: 8, core: 2. Of those that a mesh axis runs over, the one named last changes fastest.
Arguments:
- sphere_index: int32 [12288], P('grid'), may hold values from 0 to 16383, as said below
- occupied: float32 [512, 2, 12288], P('band', None, 'grid'), may hold values from -6 to 6
- energies: float32 [32], P('band'), may hold values from -3 to -0.2
- local_pot: float32 [64, 4096], P('grid'), may hold values from 0.5 to 4
- trial_pot: float32 [4, 64, 4096], P(None, 'grid'), may hold values from -24 to 24
Outputs:
- delta_psi: float32 [32, 4, 2, 12288], P('band', None, None, 'grid')
- density: float32 [4, 64, 4096], P(None, 'grid', 'band')
Inputs may be any that keep to these rules, and one draw needn't show every extreme that they name: `sphere_index`: for each grid slab g, the 768 entries from g * (768) on are distinct positions p = (kz * 4 + xl) * 64 + ky of that slab, namely those with the smallest f(kx)^2 + f(ky)^2 + f(kz)^2 where kx = g + 16 * xl, listed by rising value with ties broken at random.
All inputs are finite; a program needn't handle non-finite values.
Results may differ from a plain program's by a relative error of at most 0.0001.
Values sent between devices are 32-bit elements; how exact they have to be, the bound alone decides.
A program may use at most 128 MiB of HBM per device.

v0:
```python
import math

import jax
import jax.numpy as jnp
from jax import lax
from jax.sharding import PartitionSpec as P

NG = 64
NPW = 12288
ITERS = 2


KIN_SCALE = 0.02
SHIFT_WEIGHT = 2.0
PRECISE = lax.Precision.HIGHEST


def phase_tables(points, output_index, input_index):
    products_mod = output_index[:, None] * input_index[None, :] % points
    angles = products_mod.astype(jnp.float32) * (2.0 * math.pi / points)
    factor = 1.0 / math.sqrt(points)
    return (jnp.cos(angles) * factor, jnp.sin(angles) * factor)


def complex_table(cos_table, sin_table, sign):
    upper = jnp.stack([cos_table, -sign * sin_table])
    lower = jnp.stack([sign * sin_table, cos_table])
    return jnp.stack([upper, lower])


def swap_pair(vector):
    return jnp.stack([vector[:, 1], -vector[:, 0]], axis=1)


def wave_number(wave_index, points):
    return jnp.where(wave_index < points // 2, wave_index, wave_index - points)


def split_parts(field):
    shape = field.shape
    return field.reshape(shape[:-1] + (2, shape[-1] // 2))


def join_parts(field):
    shape = field.shape
    return field.reshape(shape[:-2] + (shape[-2] * shape[-1],))


def planes_from(spectral, tables, regroup):
    z_fwd, z_back, x_fwd, x_back, y_out, y_back = tables
    sectioned = jnp.einsum("oirk,bkxiy->brxoy", z_fwd, split_parts(spectral), precision=PRECISE)
    sectioned = regroup(join_parts(sectioned))
    sectioned = jnp.einsum("oirq,bzqiy->bzroy", x_fwd, split_parts(sectioned), precision=PRECISE)
    return jnp.einsum("bzxi,io->bzxo", join_parts(sectioned), y_out, precision=PRECISE)


def spectrum_from(real_field, tables, regroup):
    z_fwd, z_back, x_fwd, x_back, y_out, y_back = tables
    sectioned = jnp.einsum("bzxi,io->bzxo", real_field, y_back, precision=PRECISE)
    sectioned = jnp.einsum("oirq,bzriy->bzqoy", x_back, split_parts(sectioned), precision=PRECISE)
    sectioned = regroup(join_parts(sectioned))
    sectioned = jnp.einsum("oirk,brxiy->bkxoy", z_back, split_parts(sectioned), precision=PRECISE)
    return join_parts(sectioned)


def on_device(sphere_index, occupied, energies, local_pot, trial_pot):
    grid_count = lax.axis_size("grid")
    grid_rank = lax.axis_index("grid")
    band_rank = lax.axis_index("band")
    row_count = NG // grid_count
    band_count = energies.shape[0]
    pert_count = trial_pot.shape[0]
    pair_count = band_count * pert_count
    basis_norm = 2.0 * NPW
    wave_z = sphere_index // (row_count * NG)
    row_local = sphere_index // NG % row_count
    wave_y = sphere_index % NG
    wave_x = grid_rank + grid_count * row_local
    kinetic = KIN_SCALE * (
        wave_number(wave_x, NG) ** 2 + wave_number(wave_y, NG) ** 2 + wave_number(wave_z, NG) ** 2
    ).astype(jnp.float32)
    real_slot = (wave_z * row_count + row_local) * (2 * NG) + wave_y
    imag_slot = real_slot + NG
    natural = jnp.arange(NG, dtype=jnp.int32)
    placed = natural // row_count + grid_count * (natural % row_count)
    z_cos, z_sin = phase_tables(NG, natural, natural)
    x_cos, x_sin = phase_tables(NG, natural, placed)
    y_out = jnp.concatenate(
        [jnp.concatenate([z_cos, z_sin], axis=1), jnp.concatenate([-z_sin, z_cos], axis=1)], axis=0
    )
    y_back = jnp.concatenate(
        [jnp.concatenate([z_cos, -z_sin], axis=1), jnp.concatenate([z_sin, z_cos], axis=1)], axis=0
    )
    tables = (
        complex_table(z_cos, z_sin, 1.0),
        complex_table(z_cos, z_sin, -1.0),
        complex_table(x_cos, x_sin, 1.0),
        complex_table(x_cos, x_sin, -1.0),
        y_out,
        y_back,
    )
    potential = local_pot.reshape(row_count, NG, NG)
    potential = jnp.concatenate([potential, potential], axis=-1)
    trials = trial_pot.reshape(pert_count, row_count, NG, NG)
    trials = jnp.concatenate([trials, trials], axis=-1)

    def spread(coeffs):
        flattened = jnp.zeros((coeffs.shape[0], NG * row_count * 2 * NG), jnp.float32)
        flattened = flattened.at[:, real_slot].set(coeffs[:, 0]).at[:, imag_slot].set(coeffs[:, 1])
        return flattened.reshape(coeffs.shape[0], NG, row_count, 2 * NG)

    def pick_sphere(spectral):
        flattened = spectral.reshape(spectral.shape[0], -1)
        return jnp.stack([flattened[:, real_slot], flattened[:, imag_slot]], axis=1)

    everyone = lax.all_gather(occupied, "band", axis=0, tiled=True)
    own_bands = lax.dynamic_slice_in_dim(everyone, band_rank * band_count, band_count, 0)

    def correlation_terms(vector):
        count = vector.shape[0]
        both = jnp.concatenate([vector, swap_pair(vector)], axis=0)
        correlations = jnp.einsum("bkj,okj->bo", both, everyone, precision=PRECISE)
        return (correlations[:count], correlations[count:])

    def expand(correlation_re, correlation_im):
        count = correlation_re.shape[0]
        both = jnp.concatenate([correlation_re, correlation_im], axis=0)
        spread_back = jnp.einsum("bo,okj->bkj", both, everyone, precision=PRECISE)
        direct = spread_back[:count]
        turned = spread_back[count:]
        return (direct + jnp.stack([-turned[:, 1], turned[:, 0]], axis=1)) / basis_norm

    def band_group(sectioned):
        return lax.all_to_all(sectioned, "grid", split_axis=1, concat_axis=2, tiled=True)

    def source_group(sectioned):
        return lax.all_to_all(sectioned, "grid", split_axis=2, concat_axis=1, tiled=True)

    def direction_group(sectioned):
        return lax.all_to_all(sectioned, "grid", split_axis=1, concat_axis=2, tiled=True)

    def return_group(sectioned):
        return lax.all_to_all(sectioned, "grid", split_axis=2, concat_axis=1, tiled=True)

    def response_group(sectioned):
        return lax.all_to_all(sectioned, "grid", split_axis=1, concat_axis=2, tiled=True)

    def squared(vector):
        return lax.psum(jnp.sum(vector * vector, axis=(1, 2)), "grid")

    own_real = planes_from(spread(own_bands), tables, band_group)
    product = (own_real[:, None] * trials[None]).reshape(pair_count, row_count, NG, 2 * NG)
    source = pick_sphere(spectrum_from(product, tables, source_group))
    local_re, local_im = correlation_terms(source)
    correlation_re, correlation_im = lax.psum((local_re, local_im), "grid")
    right_side = expand(correlation_re, correlation_im) - source
    band_shift = jnp.repeat(energies, pert_count)[:, None, None]
    solution = jnp.zeros_like(right_side)
    residual = right_side
    direction = right_side
    norm_now = squared(residual)
    images = []
    step_sizes = []
    for iteration in range(ITERS):
        dir_real = planes_from(spread(direction), tables, direction_group)
        potential_term = pick_sphere(
            spectrum_from(dir_real * potential[None], tables, return_group)
        )
        applied = kinetic * direction + potential_term - band_shift * direction
        local_re, local_im = correlation_terms(direction)
        correlation_re, correlation_im = lax.psum((local_re, local_im), "grid")
        image = applied + SHIFT_WEIGHT * expand(correlation_re, correlation_im)
        curvature = lax.psum(jnp.sum(direction * image, axis=(1, 2)), "grid")
        step_size = norm_now / curvature
        solution = solution + step_size[:, None, None] * direction
        residual = residual - step_size[:, None, None] * image
        images.append(dir_real)
        step_sizes.append(step_size)
        if iteration + 1 < ITERS:
            norm_next = squared(residual)
            direction = residual + (norm_next / norm_now)[:, None, None] * direction
            norm_now = norm_next
    response = planes_from(spread(solution), tables, response_group)
    weighted = response.reshape(band_count, pert_count, row_count, NG, 2 * NG) * own_real[:, None]
    density_term = 2.0 * jnp.sum(weighted[..., :NG] + weighted[..., NG:], axis=0)
    density_term = density_term.reshape(pert_count, row_count, NG * NG)
    density = lax.psum_scatter(density_term, "band", scatter_dimension=2, tiled=True)
    return (solution.reshape(band_count, pert_count, 2, -1), density)


def solution(mesh):
    return jax.shard_map(
        on_device,
        mesh=mesh,
        in_specs=(
            P("grid"),
            P("band", None, "grid"),
            P("band"),
            P("grid", None),
            P(None, "grid", None),
        ),
        out_specs=(P("band", None, None, "grid"), P(None, "grid", "band")),
        check_vma=False,
    )
```

profile of v0, /device:TPU:1, one launch (start us, length us, event | category | flops | bytes accessed | tf_op | source)
XLA Modules:
  0.0 1025.4 jit_solution(18425685500949380417)
XLA Ops:
  13.7 85.0 %all-gather.2.cloned.1.call-done = f32[512,2,768]{2,0,1:T(8,128)} async-done(((f32[16,2,768]{2,0,1:T(8,128)}), f32[512,2,768]{2,0,1:T(8,128)}) %all-gather.2.cloned.1.call-update) | async-done | bytes 3145744 | tf_op jit(solution)/shard_map/all_gather | solution.py:116
  99.5 3.4 scatter_custom_fusion
  102.9 3.5 scatter_fusion
  108.0 11.5 %all-to-all-start = ((f32[1,64,4,128]{3,2,0,1:T(4,128)}), f32[1,64,4,128]{3,2,0,1:T(4,128)}, u32[]{:S(2)}, u32[]{:S(2)}) async-start(f32[1,64,4,128]{3,2,0,1:T(4,128)} %copy.90), calls=%async_computation | async-start | bytes 262144 | tf_op jit(solution)/shard_map/all_to_all | solution.py:134
  120.3 8.4 all-to-all-done
  135.1 3.0 convolution_bitcast_fusion
  138.0 2.9 fusion.39
  140.9 2.4 copy.97
  143.3 4.6 all-to-all-start.1
  147.9 16.8 %all-to-all-done.1 = f32[4,4,64,128]{3,1,0,2:T(4,128)} async-done(((f32[4,4,64,128]{3,1,0,2:T(4,128)}), f32[4,4,64,128]{3,1,0,2:T(4,128)}, u32[]{:S(2)}, u32[]{:S(2)}) %all-to-all-start.1) | async-done | bytes 524320 | tf_op jit(solution)/shard_map/all_to_all | solution.py:137
  166.9 2.7 reshape.368
  169.6 4.1 convolution_bitcast_fusion.3
  173.7 14.9 %copy.218 = f32[4,64,4,2,64]{0,4,3,2,1:T(8,128)} copy(f32[4,64,4,2,64]{1,4,3,2,0:T(8,128)} %convolution_bitcast_fusion.3) | data formatting | bytes 1048576 | tf_op jit(solution)/shard_map/reshape;reshape | solution.py:113
  188.6 8.0 gather_fusion
  198.4 8.0 gather_fusion.1
  207.6 3.4 convolution_bitcast_fusion.6
  211.6 42.5 %all-reduce.3 = (f32[4,512]{1,0:T(4,128)S(1)}, f32[4,512]{1,0:T(4,128)S(1)}) all-reduce(f32[4,512]{1,0:T(4,128)} %get-tuple-element.56, f32[4,512]{1,0:T(4,128)S(1)} %get-tuple-element.55), channel_id=1, replica_groups=mesh['band'=32,'grid'=16] {'grid'}, use_global_device_ids=true, to_apply=%region_3.4 | all-reduce | flops 4096 | bytes 32768 | tf_op jit(solution)/shard_map/psum | solution.py:155
  259.2 11.5 %scatter_custom_fusion.2 = f32[4,32768]{0,1:T(8,128)} fusion(s32[768]{0:T(1024)} %copy-done.21, f32[768,4]{1,0:T(8,128)} %copy.106, f32[]{:T(128)} %constant.113.clone.1), kind=kCustom, calls=%fused_computation.18 | custom fusion | bytes 524800 | tf_op jit(solution)/shard_map/scatter | solution.py:109
  272.3 16.0 %scatter_fusion.1 = f32[4,32768]{0,1:T(8,128)} fusion(f32[4,32768]{0,1:T(8,128)} %scatter_custom_fusion.2, s32[768]{0:T(1024)} %copy-done.14, f32[768,4]{1,0:T(8,128)} %copy.107), kind=kCustom, calls=%fused_computation.9 | custom fusion | bytes 39936 | tf_op jit(solution)/shard_map/scatter | solution.py:109
  288.3 12.9 %copy.165 = f32[4,64,4,2,64,1]{1,4,3,5,2,0:T(8,128)} copy(f32[4,64,4,2,64,1]{0,4,3,2,1,5:T(8,128)} %bitcast.311) | data formatting | bytes 1048576 | tf_op jit(solution)/shard_map/reshape;reshape | solution.py:41
  301.2 3.2 fusion.33
  304.4 2.4 copy.109
  306.8 9.0 all-to-all-start.2
  321.2 12.1 %all-to-all-done.2 = f32[4,64,4,128]{3,2,0,1:T(4,128)} async-done(((f32[4,64,4,128]{3,2,0,1:T(4,128)}), f32[4,64,4,128]{3,2,0,1:T(4,128)}, u32[]{:S(2)}, u32[]{:S(2)}) %all-to-all-start.2) | async-done | bytes 524320 | tf_op jit(solution)/shard_map/all_to_all | solution.py:140
  335.6 2.7 reshape.370
  338.3 3.0 fusion.13
  341.4 2.7 convolution_multiply_fusion.2
  345.8 2.9 fusion.38
  348.7 2.4 copy.115
  351.1 4.1 all-to-all-start.3
  355.2 3.4 convolution_bitcast_fusion.5
  359.3 45.3 %all-reduce.2 = (f32[4,512]{1,0:T(4,128)}, f32[4,512]{1,0:T(4,128)}) all-reduce(f32[4,512]{1,0:T(4,128)} %get-tuple-element.54, f32[4,512]{1,0:T(4,128)} %get-tuple-element.53), channel_id=1, replica_groups=mesh['band'=32,'grid'=16] {'grid'}, use_global_device_ids=true, to_apply=%region_9.10 | all-reduce | flops 4096 | bytes 32768 | tf_op jit(solution)/shard_map/psum | solution.py:171
  410.3 2.7 reshape.375
  413.0 4.1 convolution_bitcast_fusion.2
  417.1 14.9 %copy.220 = f32[4,64,4,2,64]{0,4,3,2,1:T(8,128)} copy(f32[4,64,4,2,64]{1,4,3,2,0:T(8,128)} %convolution_bitcast_fusion.2) | data formatting | bytes 1048576 | tf_op jit(solution)/shard_map/reshape;reshape | solution.py:113
  432.0 8.2 gather_fusion.3
  440.2 8.2 gather_fusion.2
  454.2 27.1 %all-reduce.1 = (f32[4]{0:T(128)}, f32[4]{0:T(128)}) all-reduce(f32[4]{0:T(128)} %get-tuple-element.11, f32[4]{0:T(128)} %get-tuple-element.10), channel_id=1, replica_groups=mesh['band'=32,'grid'=16] {'grid'}, use_global_device_ids=true, to_apply=%region_5.6 | all-reduce | flops 8 | bytes 64 | tf_op jit(solution)/shard_map/psum | solution.py:149
  484.0 23.7 %psum.76 = f32[4]{0:T(128)S(1)} all-reduce(f32[4]{0:T(128)} %multiply_reduce_fusion), channel_id=1, replica_groups=mesh['band'=32,'grid'=16] {'grid'}, use_global_device_ids=true, to_apply=%region_13.14 | all-reduce | flops 4 | bytes 32 | tf_op jit(solution)/shard_map/psum | solution.py:149
  512.1 11.5 %scatter_custom_fusion.4 = f32[4,32768]{0,1:T(8,128)} fusion(s32[768]{0:T(1024)} %copy-done.21, f32[768,4]{1,0:T(8,128)} %copy.124, f32[]{:T(128)} %constant.113.clone.1), kind=kCustom, calls=%fused_computation.16 | custom fusion | bytes 524800 | tf_op jit(solution)/shard_map/scatter | solution.py:109
  525.2 16.0 %scatter_fusion.2 = f32[4,32768]{0,1:T(8,128)} fusion(f32[4,32768]{0,1:T(8,128)} %scatter_custom_fusion.4, s32[768]{0:T(1024)} %copy-done.14, f32[768,4]{1,0:T(8,128)} %copy.125), kind=kCustom, calls=%fused_computation.11 | custom fusion | bytes 39936 | tf_op jit(solution)/shard_map/scatter | solution.py:109
  541.2 12.9 %copy.178 = f32[4,64,4,2,64,1]{1,4,3,5,2,0:T(8,128)} copy(f32[4,64,4,2,64,1]{0,4,3,2,1,5:T(8,128)} %bitcast.312) | data formatting | bytes 1048576 | tf_op jit(solution)/shard_map/reshape;reshape | solution.py:41
  554.2 3.2 fusion.31
  559.7 27.0 %all_to_all.105 = f32[4,64,4,128]{3,2,0,1:T(4,128)S(1)} all-to-all(f32[4,64,4,128]{3,2,0,1:T(4,128)} %copy.127), channel_id=1, replica_groups=mesh['band'=32,'grid'=16] {'grid'}, dimensions={1} | all-to-all | bytes 1048576 | tf_op jit(solution)/shard_map/all_to_all | solution.py:140
  588.1 2.7 reshape.377
  590.8 3.0 fusion.10
  593.8 2.7 convolution_multiply_fusion.1
  598.3 2.9 fusion.37
  603.5 4.1 all-to-all-start.5
  608.2 3.4 convolution_bitcast_fusion.4
  612.2 44.9 %all-reduce = (f32[4,512]{1,0:T(4,128)}, f32[4,512]{1,0:T(4,128)}) all-reduce(f32[4,512]{1,0:T(4,128)} %get-tuple-element.52, f32[4,512]{1,0:T(4,128)} %get-tuple-element.51), channel_id=1, replica_groups=mesh['band'=32,'grid'=16] {'grid'}, use_global_device_ids=true, to_apply=%region_17.18 | all-reduce | flops 4096 | bytes 32768 | tf_op jit(solution)/shard_map/psum | solution.py:171
  662.1 2.7 convolution_bitcast_fusion.1
  664.9 14.1 %copy.222 = f32[4,64,4,2,64]{0,4,3,2,1:T(8,128)} copy(f32[4,64,4,2,64]{1,4,3,2,0:T(8,128)S(1)} %convolution_bitcast_fusion.1) | data formatting | bytes 1048576 | tf_op jit(solution)/shard_map/reshape;reshape | solution.py:113
  678.9 7.3 gather_fusion.5
  686.3 7.3 gather_fusion.4
  694.1 26.4 %psum.79 = f32[4]{0:T(128)S(1)} all-reduce(f32[4]{0:T(128)S(1)} %fusion.105), channel_id=1, replica_groups=mesh['band'=32,'grid'=16] {'grid'}, use_global_device_ids=true, to_apply=%region_19.20 | all-reduce | flops 4 | bytes 32 | tf_op jit(solution)/shard_map/psum | solution.py:173
  720.8 11.2 %scatter_custom_fusion.6 = f32[4,32768]{0,1:T(8,128)} fusion(s32[768]{0:T(1024)} %copy-done.21, f32[768,4]{1,0:T(8,128)S(1)} %copy.142, f32[]{:T(128)} %constant.113.clone.1), kind=kCustom, calls=%fused_computation.14 | custom fusion | bytes 524800 | tf_op jit(solution)/shard_map/scatter | solution.py:109
  732.3 15.6 %scatter_fusion.3 = f32[4,32768]{0,1:T(8,128)} fusion(f32[4,32768]{0,1:T(8,128)} %scatter_custom_fusion.6, s32[768]{0:T(1024)S(1)} %copy-done.15, f32[768,4]{1,0:T(8,128)S(1)} %copy.143), kind=kCustom, calls=%fused_computation.13 | custom fusion | bytes 39936 | tf_op jit(solution)/shard_map/scatter | solution.py:109
  747.9 12.0 %copy.187 = f32[4,64,4,2,64,1]{1,4,3,5,2,0:T(8,128)S(1)} copy(f32[4,64,4,2,64,1]{0,4,3,2,1,5:T(8,128)} %bitcast.310) | data formatting | bytes 1048576 | tf_op jit(solution)/shard_map/reshape;reshape | solution.py:41
  761.3 26.8 %all_to_all.106 = f32[4,64,4,128]{3,2,0,1:T(4,128)S(1)} all-to-all(f32[4,64,4,128]{3,2,0,1:T(4,128)S(1)} %copy.145), channel_id=1, replica_groups=mesh['band'=32,'grid'=16] {'grid'}, dimensions={1} | all-to-all | bytes 1048576 | tf_op jit(solution)/shard_map/all_to_all | solution.py:146
  791.2 2.7 fusion.6
  794.2 6.1 copy.224
  800.3 7.6 reshape.565
  808.5 208.2 %reduce-scatter.4.cloned.1.call-done = f32[128,16]{1,0:T(8,128)} async-done(((f32[4096,16]{1,0:T(8,128)}), f32[128,16]{1,0:T(8,128)}) %reduce-scatter.4.cloned.1.call-update) | async-done | bytes 8208
  (145 shorter events, 79.5 us)
Async XLA Ops:
  7.2 91.5 %all-gather.2.cloned.1.call-start = ((), (), s32[]{:S(2)}) async-start(), calls=%async_computation.8 | async-start | bytes 3244032 | tf_op jit(solution)/shard_map/all_gather | solution.py:116
  13.6 175.0 %copy-start.14 = (s32[768]{0:T(1024)}, s32[768]{0:T(1024)S(1)}, u32[]{:S(2)}) copy-start(s32[768]{0:T(1024)S(1)} %get-tuple-element.21) | copy-start | bytes 9220
  13.6 174.9 %copy-start.21 = (s32[768]{0:T(1024)}, s32[768]{0:T(1024)S(1)}, u32[]{:S(2)}) copy-start(s32[768]{0:T(1024)S(1)} %compare_select_fusion.4) | copy-start | bytes 9220
  108.0 20.8 %all-to-all-start = ((f32[1,64,4,128]{3,2,0,1:T(4,128)}), f32[1,64,4,128]{3,2,0,1:T(4,128)}, u32[]{:S(2)}, u32[]{:S(2)}) async-start(f32[1,64,4,128]{3,2,0,1:T(4,128)} %copy.90), calls=%async_computation | async-start | bytes 262144 | tf_op jit(solution)/shard_map/all_to_all | solution.py:134
  120.3 87.2 %copy-start = (f32[512,2,768]{2,0,1:T(8,128)S(1)}, f32[512,2,768]{2,0,1:T(8,128)}, u32[]{:S(2)}) copy-start(f32[512,2,768]{2,0,1:T(8,128)} %all-gather.2.cloned.1.call-done) | copy-start | bytes 9437188
  134.4 0.6 copy-start.1
  143.3 21.5 %all-to-all-start.1 = ((f32[4,4,64,128]{3,1,0,2:T(4,128)}), f32[4,4,64,128]{3,1,0,2:T(4,128)}, u32[]{:S(2)}, u32[]{:S(2)}) async-start(f32[4,4,64,128]{3,1,0,2:T(4,128)} %copy.97), calls=%async_computation.1 | async-start | bytes 1048576 | tf_op jit(solution)/shard_map/all_to_all | solution.py:137
  147.9 40.7 %copy-start.16 = (s32[1024]{0:T(1024)}, s32[1024]{0:T(1024)S(1)}, u32[]{:S(2)}) copy-start(s32[1024]{0:T(1024)S(1)} %pad_clamp_fusion.1) | copy-start | bytes 12292
  147.9 59.6 %copy-start.18 = (s32[1024]{0:T(1024)}, s32[1024]{0:T(1024)S(1)}, u32[]{:S(2)}) copy-start(s32[1024]{0:T(1024)S(1)} %pad_clamp_fusion) | copy-start | bytes 12292
  255.7 0.6 copy-start.2
  255.7 226.3 %copy-start.4 = (f32[4,1,768]{2,0,1:T(4,128)}, f32[4,1,768]{2,0,1:T(4,128)S(1)}, u32[]{:S(2)}) copy-start(f32[4,1,768]{2,0,1:T(4,128)S(1)} %get-tuple-element.35) | copy-start | bytes 36868
  255.7 226.3 %copy-start.6 = (f32[4,1,768]{2,0,1:T(4,128)}, f32[4,1,768]{2,0,1:T(4,128)S(1)}, u32[]{:S(2)}) copy-start(f32[4,1,768]{2,0,1:T(4,128)S(1)} %get-tuple-element.36) | copy-start | bytes 36868
  256.3 0.6 copy-start.8
  306.8 26.5 %all-to-all-start.2 = ((f32[4,64,4,128]{3,2,0,1:T(4,128)}), f32[4,64,4,128]{3,2,0,1:T(4,128)}, u32[]{:S(2)}, u32[]{:S(2)}) async-start(f32[4,64,4,128]{3,2,0,1:T(4,128)} %copy.109), calls=%async_computation.2 | async-start | bytes 1048576 | tf_op jit(solution)/shard_map/all_to_all | solution.py:140
  351.1 57.1 %all-to-all-start.3 = ((f32[4,4,64,128]{3,1,0,2:T(4,128)}), f32[4,4,64,128]{3,1,0,2:T(4,128)}, u32[]{:S(2)}, u32[]{:S(2)}) async-start(f32[4,4,64,128]{3,1,0,2:T(4,128)} %copy.115), calls=%async_computation.3 | async-start | bytes 1048576 | tf_op jit(solution)/shard_map/all_to_all | solution.py:143
  406.9 0.6 copy-start.13
  482.0 0.5 copy-start.22
  507.7 0.6 copy-start.24
  603.5 56.5 %all-to-all-start.5 = ((f32[4,4,64,128]{3,1,0,2:T(4,128)}), f32[4,4,64,128]{3,1,0,2:T(4,128)}, u32[]{:S(2)}, u32[]{:S(2)}) async-start(f32[4,4,64,128]{3,1,0,2:T(4,128)} %copy.133), calls=%async_computation.5 | async-start | bytes 1048576 | tf_op jit(solution)/shard_map/all_to_all | solution.py:143
  607.7 409.0 %reduce-scatter.4.cloned.1.call-start = ((), (), s32[]{:S(2)}) async-start(), calls=%async_computation.9 | async-start | bytes 2162688
  659.4 0.6 copy-start.11
  660.0 18.9 %copy-start.19 = (s32[1024]{0:T(1024)S(1)}, s32[1024]{0:T(1024)}, u32[]{:S(2)}) copy-start(s32[1024]{0:T(1024)} %copy-done.18) | copy-start | bytes 12292
  660.0 26.2 %copy-start.17 = (s32[1024]{0:T(1024)S(1)}, s32[1024]{0:T(1024)}, u32[]{:S(2)}) copy-start(s32[1024]{0:T(1024)} %copy-done.16) | copy-start | bytes 12292
  660.0 33.9 %copy-start.20 = (f32[768]{0:T(1024)S(1)}, f32[768]{0:T(1024)}, u32[]{:S(2)}) copy-start(f32[768]{0:T(1024)} %fusion.124) | copy-start | bytes 9220
  660.0 60.5 %copy-start.25 = (f32[4]{0:T(128)S(1)}, f32[4]{0:T(128)}, u32[]{:S(2)}) copy-start(f32[4]{0:T(128)} %copy-done.24) | copy-start | bytes 52
  660.0 60.5 %copy-start.3 = (f32[8,2,768]{2,0,1:T(8,128)S(1)}, f32[8,2,768]{2,0,1:T(8,128)}, u32[]{:S(2)}) copy-start(f32[8,2,768]{2,0,1:T(8,128)} %copy-done.2) | copy-start | bytes 147460
  660.0 60.5 %copy-start.5 = (f32[4,1,768]{2,0,1:T(4,128)S(1)}, f32[4,1,768]{2,0,1:T(4,128)}, u32[]{:S(2)}) copy-start(f32[4,1,768]{2,0,1:T(4,128)} %copy-done.4) | copy-start | bytes 36868
  660.0 60.5 %copy-start.7 = (f32[4,1,768]{2,0,1:T(4,128)S(1)}, f32[4,1,768]{2,0,1:T(4,128)}, u32[]{:S(2)}) copy-start(f32[4,1,768]{2,0,1:T(4,128)} %copy-done.6) | copy-start | bytes 36868
  660.0 60.5 %copy-start.23 = (f32[4]{0:T(128)S(1)}, f32[4]{0:T(128)}, u32[]{:S(2)}) copy-start(f32[4]{0:T(128)} %copy-done.22) | copy-start | bytes 52
  660.1 33.8 %copy-start.12 = (f32[8,2,768]{2,0,1:T(8,128)S(1)}, f32[8,2,768]{2,0,1:T(8,128)}, u32[]{:S(2)}) copy-start(f32[8,2,768]{2,0,1:T(8,128)} %copy-done.11) | copy-start | bytes 147460
  664.8 67.4 %copy-start.15 = (s32[768]{0:T(1024)S(1)}, s32[768]{0:T(1024)}, u32[]{:S(2)}) copy-start(s32[768]{0:T(1024)} %copy-done.14) | copy-start | bytes 9220
  720.6 39.2 %copy-start.9 = (f32[4,2,768]{2,0,1:T(4,128)}, f32[4,2,768]{2,0,1:T(4,128)S(1)}, u32[]{:S(2)}) copy-start(f32[4,2,768]{2,0,1:T(4,128)S(1)} %multiply_add_fusion) | copy-start | bytes 73732
  760.9 47.0 %copy-start.10 = (f32[4,2,768]{2,0,1:T(4,128)S(1)}, f32[4,2,768]{2,0,1:T(4,128)}, u32[]{:S(2)}) copy-start(f32[4,2,768]{2,0,1:T(4,128)} %copy-done.9) | copy-start | bytes 73732
Sparse Core Ops, SparseCore 0:
  11.2 87.4 all-gather.1
  808.0 208.6 reduce-scatter.3
where the time goes:
time: 1040 us; the launch traced here: 1030 us
  waiting for transfers between devices  331 us (32%)
  local copies, waits for them, and re-layouts  298 us (29%)
  blocking collectives  264 us (25%)
  matrix products  68.6 us (7%)
  starting transfers between devices  33.9 us (3%)
  between operations  15.5 us (1%)
  other arithmetic  15 us (1%)
    unnamed x3, waiting for transfers between devices  208 us
    psum x3, blocking collectives, on_device(): correlation_re, correlation_im = lax.psum((local_re, local_im), 'grid')  133 us
    scatter x8, local copies, waits for them, and re-layouts, spread(): flattened.at[:, real_slot].set(coeffs[:, 0]).at[:, imag_slot]  88.7 us
    all_gather x1, waiting for transfers between devices, on_device(): everyone = lax.all_gather(occupied, 'band', axis=0, tiled=True)  85 us
    gather x12, local copies, waits for them, and re-layouts, pick_sphere(): return jnp.stack([flattened[:, real_slot], flattened[:, imag_slot]], axis=1)  53.3 us
    psum x2, blocking collectives, squared(): return lax.psum(jnp.sum(vector * vector, axis=(1, 2)), 'grid')  50.8 us
    another operation x3, local copies, waits for them, and re-layouts, pick_sphere(): flattened = spectral.reshape(spectral.shape[0], -1)  43.9 us
    another operation x3, local copies, waits for them, and re-layouts, split_parts(): return field.reshape(shape[:-1] + (2, shape[-1] // 2))  37.8 us
  transfers between devices with their start and end apart: 7, of which 5 were waited for; matrix products, arithmetic and copies ran while one was open for 2% of the time, Pallas kernels for 0%

commit v1 on v0

v1 whole, which is shorter than its diff:
```python
import numpy as np
import jax
import jax.numpy as jnp
import ml_dtypes
from jax import lax
from jax.experimental import pallas as pl
from jax.experimental.pallas import tpu as pltpu
from jax.sharding import PartitionSpec as P

NG = 64
NPW = 12288
NJ = 768
PERTS = 4
GRID = 16
XS, ZS = 4, 8
BANDS = 32
KIN_SCALE = 0.02
MESH = pl.DeviceIdType.MESH
F32 = jnp.float32
BF16 = jnp.bfloat16


def halves(table):
    high = table.astype(ml_dtypes.bfloat16)
    low = (table - high.astype(np.float64)).astype(ml_dtypes.bfloat16)
    return high, low


def make_tables():
    freq = np.arange(32) - 32 * (np.arange(32) >= 16)
    norm = 1.0 / np.sqrt(NG)
    angle = 2 * np.pi / NG
    phase = np.exp(1j * angle * np.outer(np.arange(NG), freq)) * norm
    z_tab = np.zeros((NG, 2, 2, 32))
    for ri in range(2):
        value = phase * (1j**ri)
        z_tab[:, 0, ri], z_tab[:, 1, ri] = value.real, value.imag
    z_tab = z_tab.reshape(128, 64)
    y_tab = np.zeros((PERTS, 2, 32, 2, 2, PERTS, NG))
    own_tab = np.zeros((2, 2, 32, 2, 2, PERTS, NG))
    for p in range(PERTS):
        for k in range(2):
            y_tab[p, k, :, k, 0, p] = phase.real.T
            y_tab[p, k, :, k, 1, p] = phase.imag.T
            own_tab[0, k, :, k, 0, p] = phase.real.T
            own_tab[0, k, :, k, 1, p] = phase.imag.T
    y_tab = y_tab.reshape(256, 1024)
    own_tab = own_tab.reshape(128, 1024)
    x_tab = np.zeros((2, 32, 2, 4, 2, 2, GRID, 4, 2))
    for k in range(2):
        rotor = np.exp(1j * angle * np.outer(np.arange(NG), np.arange(GRID) - 16 * k)) * norm
        rotor = rotor.reshape(32, 2, GRID)
        for cs in range(2):
            for ri in range(2):
                value = rotor * (1j ** (cs + ri))
                for zl in range(4):
                    x_tab[0, :, :, zl, k, cs, :, zl, ri] = value.real
                    x_tab[1, :, :, zl, k, cs, :, zl, ri] = value.imag
    x_tab = x_tab.reshape(512, 512)
    tables = []
    for table in (z_tab, y_tab, own_tab, x_tab, x_tab.T):
        tables.extend(halves(table))
    return tables


def split(value):
    high = value.astype(BF16)
    return high, (value - high.astype(F32)).astype(BF16)


def dot(a, b, ca, cb):
    return lax.dot_general(a, b, (((ca,), (cb,)), ((), ())), preferred_element_type=F32)


def dot3(a_high, a_low, b_high, b_low, ca=1, cb=0):
    total = dot(a_high, b_high, ca, cb) + dot(a_low, b_high, ca, cb)
    return total + dot(a_high, b_low, ca, cb)


def turn(vector):
    return jnp.concatenate([-vector[:, NJ:], vector[:, :NJ]], axis=1)


def kernel(
    sph, occ, energy, pot, trial,
    zt_hi, zt_lo, y_hi, y_lo, o_hi, o_lo, t_hi, t_lo, tt_hi, tt_lo,
    dpsi, dens,
    gath, gath_hi, gath_lo, own, ztab_hi, ztab_lo, col_mask, rhs_hi, rhs_lo,
    own_send, own_recv, send, recv, tile_send, tile_recv, full_send, full_recv, sum_send, sum_recv,
    den_send, den_recv, own_field, field, ssem, rsem, gsend, grecv,
):
    g = lax.axis_index("grid")
    r = lax.axis_index("band")
    bx, bz = r // ZS, r % ZS

    barrier = pltpu.get_barrier_semaphore()

    def greet_grid(k, carry):
        pl.semaphore_signal(barrier, inc=1, device_id={"grid": (g + k) % GRID}, device_id_type=MESH)
        return carry

    def greet_band(k, carry):
        pl.semaphore_signal(barrier, inc=1, device_id={"band": (r + k) % BANDS}, device_id_type=MESH)
        return carry

    lax.fori_loop(1, GRID, greet_grid, 0)
    lax.fori_loop(1, BANDS, greet_band, 0)

    def taken(ref, sem):
        pltpu.make_async_copy(ref, ref, sem).wait()

    def to_band(src, dst, send_sem, recv_sem, x, z):
        pltpu.make_async_remote_copy(
            src_ref=src, dst_ref=dst, send_sem=send_sem, recv_sem=recv_sem,
            device_id={"band": x * ZS + z}, device_id_type=MESH,
        ).start()

    place = sph[...]
    kz, xl, ky = place // 256, (place // 64) % 4, place % 64
    kx = g + 16 * xl

    def wave(k):
        return jnp.where(k < 32, k, k - 64)

    fx, fy, fz = wave(kx), wave(ky), wave(kz)
    kinetic = KIN_SCALE * (fx * fx + fy * fy + fz * fz).astype(F32)
    diag = jnp.concatenate([kinetic, kinetic], axis=1) - energy[0, 0]
    one_z = jnp.where(lax.broadcasted_iota(jnp.int32, (32, NJ), 0) == (kz & 31), 1.0, 0.0).astype(BF16)
    column = (xl >> 1) * 32 + (ky & 31)
    one_col = jnp.where(lax.broadcasted_iota(jnp.int32, (64, NJ), 0) == column, 1.0, 0.0)
    col_mask[:, :NJ] = one_col
    col_mask[:, NJ:] = one_col
    for ri in range(2):
        lanes = pl.ds(ri * NJ, NJ)
        ztab_hi[:, lanes] = dot(zt_hi[:, 32 * ri : 32 * ri + 32], one_z, 1, 0).astype(BF16)
        ztab_lo[:, lanes] = dot(zt_lo[:, 32 * ri : 32 * ri + 32], one_z, 1, 0).astype(BF16)
    own_z = pl.ds(pl.multiple_of(8 * bz, 8), 8)
    for part in range(2):
        for ri in range(2):
            gath[part, bx, own_z, NJ * ri : NJ * ri + NJ] = occ[8 * part : 8 * part + 8, ri, :]

    pl.semaphore_wait(barrier, GRID - 1 + BANDS - 1)

    @pl.when(r == 0)
    def _():
        pltpu.make_async_copy(occ.at[0], own, rsem.at[0]).start()

    @pl.when(r < 2)
    def _():
        def give(i, carry):
            pltpu.make_async_remote_copy(
                src_ref=occ.at[i], dst_ref=own, send_sem=ssem.at[0], recv_sem=rsem.at[0],
                device_id={"band": 16 * r + i}, device_id_type=MESH,
            ).start()
            return carry

        lax.fori_loop(jnp.where(r == 0, 1, 0), 16, give, 0)

    def block(part, x, z):
        return gath.at[part, x, pl.ds(pl.multiple_of(8 * z, 8), 8)]

    def col(z, first=0, count=XS):
        return gath.at[0, pl.ds(first, count), pl.ds(pl.multiple_of(8 * z, 8), 8)]

    z_up, z_dn = (bz + 1) % ZS, (bz + ZS - 1) % ZS

    def across(part, z, slot):
        for k in range(1, XS):
            to_band(block(part, bx, z), block(part, bx, z), gsend.at[slot], grecv.at[slot], (bx + k) % XS, bz)

    def gather_0():
        across(0, bz, 0)
        to_band(block(1, bx, bz), block(1, bx, bz), gsend.at[3], grecv.at[10], bx, z_up)
        to_band(block(1, bx, bz), block(1, bx, bz), gsend.at[3], grecv.at[11], bx, z_dn)
        across(1, bz, 1)

    def gather_1():
        taken(gath.at[0, pl.ds(0, 3), pl.ds(0, 8)], grecv.at[0])
        to_band(col(bz), col(bz), gsend.at[2], grecv.at[2], bx, z_up)
        to_band(col(bz), col(bz), gsend.at[2], grecv.at[3], bx, z_dn)
        gather_part1(1)

    def gather_part1(d):
        below, above = (bz + ZS - d) % ZS, (bz + d) % ZS
        taken(block(1, bx, below), grecv.at[8 + 2 * d])
        to_band(block(1, bx, below), block(1, bx, below), gsend.at[3], grecv.at[10 + 2 * d], bx, z_up)
        taken(block(1, bx, above), grecv.at[9 + 2 * d])
        if d < 3:
            to_band(block(1, bx, above), block(1, bx, above), gsend.at[3], grecv.at[11 + 2 * d], bx, z_dn)
        across(1, below, 1)
        across(1, above, 1)

    def gather_mid(d):
        below, above = (bz + ZS - d + 1) % ZS, (bz + d - 1) % ZS
        taken(col(below), grecv.at[2 * d - 2])
        to_band(col(below), col(below), gsend.at[2], grecv.at[2 * d], bx, z_up)
        taken(col(above), grecv.at[2 * d - 1])
        to_band(col(above), col(above), gsend.at[2], grecv.at[2 * d + 1], bx, z_dn)
        gather_part1(d)

    def gather_4():
        below, above = (bz + ZS - 3) % ZS, (bz + 3) % ZS
        taken(col(below), grecv.at[6])
        to_band(col(below, 0, 2), col(below, 0, 2), gsend.at[2], grecv.at[8], bx, z_up)
        taken(col(above), grecv.at[7])
        to_band(col(above, 2, 2), col(above, 2, 2), gsend.at[2], grecv.at[9], bx, z_dn)
        far = (bz + 4) % ZS
        taken(block(1, bx, far), grecv.at[16])
        across(1, far, 1)

    def gather_5():
        far = (bz + 4) % ZS
        taken(col(far, 0, 2), grecv.at[8])
        taken(col(far, 2, 2), grecv.at[9])
        taken(gath.at[1, pl.ds(0, 3)], grecv.at[1])

    def exchange(src, dst, slot):
        def go(k, carry):
            peer = (g + k) % GRID
            pltpu.make_async_remote_copy(
                src_ref=src.at[pl.ds(pl.multiple_of(8 * peer, 8), 8)],
                dst_ref=dst.at[pl.ds(pl.multiple_of(8 * g, 8), 8)],
                send_sem=ssem.at[slot], recv_sem=rsem.at[slot],
                device_id={"grid": peer}, device_id_type=MESH,
            ).start()
            return carry

        lax.fori_loop(1, GRID, go, 0)
        here = pl.ds(pl.multiple_of(8 * g, 8), 8)
        dst[here, :] = src[here, :]

    def exchanged(dst, slot):
        taken(dst.at[pl.ds(0, 8 * (GRID - 1))], rsem.at[slot])

    def tiles(n, slot):
        def go(k, carry):
            peer = (g + k) % GRID
            pltpu.make_async_remote_copy(
                src_ref=tile_send.at[n, peer // 4], dst_ref=tile_recv.at[n, g],
                send_sem=ssem.at[slot], recv_sem=rsem.at[slot],
                device_id={"grid": peer}, device_id_type=MESH,
            ).start()
            return carry

        lax.fori_loop(1, GRID, go, 0)
        tile_recv[n, g] = tile_send[n, g // 4]

    def tiles_sum(n, slot):
        taken(tile_recv.at[n, pl.ds(0, GRID - 1)], rsem.at[slot])
        return jnp.sum(tile_recv[n], axis=0)

    def share(n, total, slot):
        quarter = g // 4
        full_send[n] = total
        for k in range(1, 4):
            pltpu.make_async_remote_copy(
                src_ref=full_send.at[n], dst_ref=full_recv.at[n, quarter],
                send_sem=ssem.at[slot], recv_sem=rsem.at[slot],
                device_id={"grid": (g + 4 * k) % GRID}, device_id_type=MESH,
            ).start()
        full_recv[n, quarter] = total

    def shared(n, slot):
        taken(full_recv.at[n, pl.ds(0, 3)], rsem.at[slot])
        return jnp.concatenate([full_recv[n, k] for k in range(4)], axis=1)

    def sums(n, value, slot):
        sum_send[n] = value

        def go(k, carry):
            pltpu.make_async_remote_copy(
                src_ref=sum_send.at[n], dst_ref=sum_recv.at[n, g],
                send_sem=ssem.at[slot], recv_sem=rsem.at[slot],
                device_id={"grid": (g + k) % GRID}, device_id_type=MESH,
            ).start()
            return carry

        lax.fori_loop(1, GRID, go, 0)
        sum_recv[n, g] = value

    def summed(n, slot):
        taken(sum_recv.at[n, pl.ds(0, GRID - 1)], rsem.at[slot])
        return jnp.sum(sum_recv[n], axis=0)

    def spread(rows, count):
        for p in range(count):
            row = rows[p : p + 1]
            high = row.astype(BF16).astype(F32)
            mask = col_mask[...]
            rhs_hi[64 * p : 64 * p + 64, :] = (mask * high).astype(BF16)
            rhs_lo[64 * p : 64 * p + 64, :] = (mask * (row - high)).astype(BF16)
        wide = pl.ds(0, 64 * count)
        return dot3(ztab_hi[...], ztab_lo[...], rhs_hi[wide, :], rhs_lo[wide, :], 1, 1)

    def to_planes(spectral, yh, yl):
        high, low = split(spectral)
        part = dot3(high, low, yh[...], yl[...])
        part = jnp.concatenate([part[:, 256 * k : 256 * k + 256] for k in range(4)], axis=0)
        high, low = split(part)
        return dot3(t_hi[...], t_lo[...], high, low)

    def from_planes(values):
        high, low = split(values)
        part = dot3(tt_hi[...], tt_lo[...], high, low)
        part = jnp.concatenate([part[128 * k : 128 * k + 128] for k in range(4)], axis=1)
        high, low = split(part)
        return dot3(high, low, y_hi[...], y_lo[...], 1, 1)

    sub8 = lax.broadcasted_iota(jnp.int32, (8, 1), 0)

    def pick(spectral):
        high, low = split(jnp.transpose(spectral))
        result = jnp.zeros((8, 2 * NJ), F32)
        for p in range(PERTS):
            rows = slice(64 * p, 64 * p + 64)
            box = dot3(high[rows], low[rows], ztab_hi[...], ztab_lo[...])
            line = jnp.sum(box * col_mask[...], axis=0, keepdims=True)
            result = jnp.where(sub8 == p, line, result)
            result = jnp.where(sub8 == p + 4, -turn(line), result)
        return result

    def correlate(vector, n):
        high = vector.astype(BF16).astype(F32)
        both = jnp.concatenate([high, vector - high], axis=0).astype(BF16)
        first = dot(both, gath_hi[...], 1, 1)
        second = dot(both, gath_lo[...], 1, 1)
        total = first[:8] + first[8:] + second[:8]
        for k in range(4):
            tile_send[n, k] = total[:, 128 * k : 128 * k + 128]

    sign = jnp.where(sub8 < 4, 1.0, -1.0)

    def expand(correlations):
        high = correlations.astype(BF16).astype(F32)
        both = jnp.concatenate([high, correlations - high], axis=0).astype(BF16)
        first = dot(both, gath_hi[...], 1, 0)
        second = dot(both, gath_lo[...], 1, 0)
        direct = first[:8] + first[8:] + second[:8]
        return (direct + sign * turn(pltpu.roll(direct, 4, 0))) * (1.0 / (2.0 * NPW))

    def per_lane(column_values):
        which = lax.broadcasted_iota(jnp.int32, (1, 256), 1) // 64
        result = jnp.zeros((1, 256), F32)
        for p in range(PERTS):
            result = jnp.where(which == p, column_values[p : p + 1, 0:1], result)
        return result

    def over_lanes(value):
        return jnp.sum(value, axis=1, keepdims=True)

    gather_0()
    taken(own, rsem.at[0])
    own_row = jnp.concatenate([own[0:1, :], own[1:2, :]], axis=1)
    own_send[...] = spread(jnp.concatenate([own_row, own_row], axis=0), 2)
    exchange(own_send, own_recv, 1)
    gather_1()
    exchanged(own_recv, 1)
    own_field[...] = to_planes(own_recv[...], o_hi, o_lo)

    weight = trial[...]
    send[0] = from_planes(jnp.concatenate([own_field[:256] * weight, own_field[256:] * weight], axis=0))
    exchange(send.at[0], recv.at[0], 2)
    gather_mid(2)
    gather_mid(3)
    exchanged(recv.at[0], 2)
    source = pick(recv[0])
    gather_4()
    gather_5()

    def round_pair(k, carry):
        rows = pl.ds(pl.multiple_of(16 * k, 16), 16)
        high, low = split(gath[k // 16, (k // 4) % 4, pl.ds(pl.multiple_of(16 * (k % 4), 16), 16), :])
        gath_hi[rows, :] = high
        gath_lo[rows, :] = low
        return carry

    lax.fori_loop(0, 32, round_pair, 0)
    correlate(source, 0)
    tiles(0, 3)
    share(0, tiles_sum(0, 3), 4)
    direction = expand(shared(0, 4)) - source

    send[1] = spread(direction, PERTS)
    exchange(send.at[1], recv.at[1], 5)
    correlate(direction, 1)
    tiles(1, 6)
    exchanged(recv.at[1], 5)
    field[0] = to_planes(recv[1], y_hi, y_lo)
    local = pot[...]
    send[2] = from_planes(jnp.concatenate([field[0, :256] * local, field[0, 256:] * local], axis=0))
    exchange(send.at[2], recv.at[2], 7)
    corr_dir = tiles_sum(1, 6)
    share(1, corr_dir, 8)
    image = diag * direction + 2.0 * expand(shared(1, 8))
    exchanged(recv.at[2], 7)
    image = image + pick(recv[2])

    send[3] = spread(image, PERTS)
    exchange(send.at[3], recv.at[3], 9)
    lane = lax.broadcasted_iota(jnp.int32, (8, 128), 1)
    dots = jnp.where(lane == 0, over_lanes(direction * direction), 0.0)
    dots = jnp.where(lane == 1, over_lanes(direction * image), dots)
    dots = jnp.where(lane == 2, over_lanes(image * image), dots)
    sums(0, dots, 10)
    correlate(image, 2)
    tiles(2, 11)
    exchanged(recv.at[3], 9)
    field[1] = to_planes(recv[3], y_hi, y_lo)
    dots = summed(0, 10)
    norm = dots[:, 0:1]
    step0 = norm / dots[:, 1:2]
    norm_next = step0 * step0 * dots[:, 2:3] - norm
    grow = 1.0 + norm_next / norm
    direction1 = grow * direction - step0 * image
    field[1] = per_lane(grow) * field[0] - per_lane(step0) * field[1]
    corr_dir1 = grow * corr_dir - step0 * tiles_sum(2, 11)

    energy_terms = over_lanes(diag * direction1 * direction1)
    corr_terms = over_lanes(corr_dir1 * corr_dir1)
    corr_terms = corr_terms + pltpu.roll(jnp.broadcast_to(corr_terms, (8, 128)), 4, 0)[:, 0:1]
    energy_terms = energy_terms + corr_terms * (2.0 / (2.0 * NPW) / 4.0)
    real, imag = field[1, :256], field[1, 256:]
    squares = jnp.sum(local * (real * real + imag * imag), axis=0, keepdims=True)
    for p in range(PERTS):
        piece = over_lanes(squares[:, 64 * p : 64 * p + 64])
        energy_terms = energy_terms + jnp.where((sub8 % 4) == p, piece, 0.0)
    sums(1, jnp.broadcast_to(energy_terms, (8, 128)), 12)
    own_re, own_im = own_field[:256], own_field[256:]
    dens0 = own_re * field[0, :256] + own_im * field[0, 256:]
    dens1 = own_re * real + own_im * imag
    dens0 = 2.0 * per_lane(step0) * dens0
    step1 = norm_next / summed(1, 12)[:, 0:1]
    den_send[...] = dens0 + 2.0 * per_lane(step1) * dens1

    def give_density(k, carry):
        peer = (r + k) % BANDS
        pltpu.make_async_remote_copy(
            src_ref=den_send.at[pl.ds(pl.multiple_of(8 * peer, 8), 8)],
            dst_ref=den_recv.at[pl.ds(pl.multiple_of(8 * r, 8), 8)],
            send_sem=ssem.at[13], recv_sem=rsem.at[13],
            device_id={"band": peer}, device_id_type=MESH,
        ).start()
        return carry

    lax.fori_loop(1, BANDS, give_density, 0)
    here = pl.ds(pl.multiple_of(8 * r, 8), 8)
    den_recv[here, :] = den_send[here, :]
    response = step0 * direction + step1 * direction1
    for ri in range(2):
        dpsi[0, :, ri, :] = response[:PERTS, NJ * ri : NJ * ri + NJ]

    @pl.when(r == 0)
    def _():
        taken(occ.at[pl.ds(0, 15)], ssem.at[0])

    @pl.when(r == 1)
    def _():
        taken(occ, ssem.at[0])

    taken(own_send.at[pl.ds(0, 120)], ssem.at[1])
    for n, slot in ((0, 2), (1, 5), (2, 7), (3, 9)):
        taken(send.at[n, pl.ds(0, 120)], ssem.at[slot])
    for n, slot in ((0, 3), (1, 6), (2, 11)):
        taken(tile_recv.at[n, pl.ds(0, 15)], ssem.at[slot])
    for n, slot in ((0, 4), (1, 8)):
        taken(full_recv.at[n, pl.ds(0, 3)], ssem.at[slot])
    for n, slot in ((0, 10), (1, 12)):
        taken(sum_recv.at[n, pl.ds(0, 15)], ssem.at[slot])
    taken(gath.at[0, pl.ds(0, 3), pl.ds(0, 8)], gsend.at[0])
    taken(gath.at[1, pl.ds(0, 3)], gsend.at[1])
    taken(gath.at[0, :, pl.ds(0, 56)], gsend.at[2])
    taken(gath.at[0, 0, pl.ds(0, 56)], gsend.at[3])

    taken(den_recv.at[pl.ds(0, 8 * (BANDS - 1))], rsem.at[13])
    total = jnp.zeros((8, 256), F32)
    for k in range(BANDS):
        total = total + den_recv[8 * k : 8 * k + 8, :]
    for p in range(PERTS):
        for half in range(2):
            dens[p, :, 64 * half : 64 * half + 64] = total[4 * half : 4 * half + 4, 64 * p : 64 * p + 64]
    taken(den_send.at[pl.ds(0, 8 * (BANDS - 1))], ssem.at[13])


def on_device(sphere_index, occupied, energies, local_pot, trial_pot):
    trial = trial_pot.reshape(PERTS, 4, 32, 2, NG).transpose(2, 3, 1, 0, 4).reshape(256, 256)
    pot = local_pot.reshape(4, 32, 2, 1, NG).transpose(1, 2, 0, 3, 4)
    pot = jnp.broadcast_to(pot, (32, 2, 4, PERTS, NG)).reshape(256, 256)
    tables = [jnp.asarray(table) for table in make_tables()]
    vmem = pl.BlockSpec(memory_space=pltpu.VMEM)
    smem = pl.BlockSpec(memory_space=pltpu.SMEM)
    scratch = [
        pltpu.VMEM((2, XS, 64, 2 * NJ), F32),
        pltpu.VMEM((512, 2 * NJ), BF16),
        pltpu.VMEM((512, 2 * NJ), BF16),
        pltpu.VMEM((2, NJ), F32),
        pltpu.VMEM((128, 2 * NJ), BF16),
        pltpu.VMEM((128, 2 * NJ), BF16),
        pltpu.VMEM((64, 2 * NJ), F32),
        pltpu.VMEM((256, 2 * NJ), BF16),
        pltpu.VMEM((256, 2 * NJ), BF16),
        pltpu.VMEM((128, 128), F32),
        pltpu.VMEM((128, 128), F32),
        pltpu.VMEM((4, 128, 256), F32),
        pltpu.VMEM((4, 128, 256), F32),
        pltpu.VMEM((3, 4, 8, 128), F32),
        pltpu.VMEM((3, GRID, 8, 128), F32),
        pltpu.VMEM((2, 8, 128), F32),
        pltpu.VMEM((2, 4, 8, 128), F32),
        pltpu.VMEM((2, 8, 128), F32),
        pltpu.VMEM((2, GRID, 8, 128), F32),
        pltpu.VMEM((256, 256), F32),
        pltpu.VMEM((256, 256), F32),
        pltpu.VMEM((512, 256), F32),
        pltpu.VMEM((2, 512, 256), F32),
        pltpu.SemaphoreType.DMA((14,)),
        pltpu.SemaphoreType.DMA((14,)),
        pltpu.SemaphoreType.DMA((4,)),
        pltpu.SemaphoreType.DMA((17,)),
    ]
    return pl.pallas_call(
        kernel,
        out_shape=(
            jax.ShapeDtypeStruct((1, PERTS, 2, NJ), F32),
            jax.ShapeDtypeStruct((PERTS, 4, 128), F32),
        ),
        in_specs=[vmem, vmem, smem] + [vmem] * 12,
        out_specs=(vmem, vmem),
        scratch_shapes=scratch,
        compiler_params=pltpu.CompilerParams(
            collective_id=0, has_side_effects=True, vmem_limit_bytes=56 * 1024 * 1024
        ),
        name="response",
    )(sphere_index.reshape(1, NJ), occupied, energies.reshape(1, 1), pot, trial, *tables)


def solution(mesh):
    return jax.shard_map(
        on_device,
        mesh=mesh,
        in_specs=(
            P("grid"),
            P("band", None, "grid"),
            P("band"),
            P("grid", None),
            P(None, "grid", None),
        ),
        out_specs=(P("band", None, None, "grid"), P(None, "grid", "band")),
        check_vma=False,
    )
```

time: 1040 us -> 115 us (0.11); the launches traced: 1030 us -> 115 us
  waiting for transfers between devices: 331 us -> 0 us
  local copies, waits for them, and re-layouts: 298 us -> 6.69 us
  blocking collectives: 264 us -> 0 us
  Pallas kernels: 0 us -> 107 us
  matrix products: 68.6 us -> 0 us
  starting transfers between devices: 33.9 us -> 0 us
  other arithmetic: 15 us -> 0 us
  between operations: 15.5 us -> 1.34 us
    psum x6 -> x0, blocking collectives: 210 us -> none  [the longest x3 133 us: on_device(): correlation_re, correlation_im = lax.psum((local_re, local_im), 'grid')]
    unnamed x3 -> x0, waiting for transfers between devices: 208 us -> none
    pallas_call x0 -> x1, Pallas kernels: none -> 107 us  [on_device(): pl.pallas_call(kernel, out_shape=(jax.ShapeDtypeStruct((1, PERTS, 2, NJ),...]
    scatter x8 -> x0, local copies, waits for them, and re-layouts: 88.7 us -> none  [spread(): flattened.at[:, real_slot].set(coeffs[:, 0]).at[:, imag_slot]]
    all_gather x1 -> x0, waiting for transfers between devices: 85 us -> none  [on_device(): everyone = lax.all_gather(occupied, 'band', axis=0, tiled=True)]
    another operation x7 -> x0, local copies, waits for them, and re-layouts: 83.5 us -> none  [the longest x3 43.9 us: pick_sphere(): flattened = spectral.reshape(spectral.shape[0], -1)]
    dot_general x25 -> x0, matrix products: 65.2 us -> none  [the longest x3 10.9 us: spectrum_from(): jnp.einsum('oirk,brxiy->bkxoy', z_back, split_parts(sectioned), precision...]
    all_to_all x2 -> x0, blocking collectives: 53.9 us -> none  [the longest x1 27 us: direction_group(): lax.all_to_all(sectioned, 'grid', split_axis=1, concat_axis=2, tiled=True)]
  transfers between devices with their start and end apart: 7 -> 0, of which waited for: 5 -> 0; matrix products, arithmetic and copies ran while one was open for 2% -> 0% of each run, Pallas kernels for 0% -> 0%
where the time goes in v1:
time: 115 us
  Pallas kernels  107 us (93%)
  local copies, waits for them, and re-layouts  6.69 us (6%)
  between operations  1.34 us (1%)
    pallas_call x1, Pallas kernels, on_device(): pl.pallas_call(kernel, out_shape=(jax.ShapeDtypeStruct((1, PERTS, 2, NJ),...  107 us
    reshape x3, local copies, waits for them, and re-layouts, on_device(): trial_pot.reshape(PERTS, 4, 32, 2, NG).transpose(2, 3, 1, 0, 4)  2.75 us

profile of v1, /device:TPU:1, one launch (start us, length us, event | category | flops | bytes accessed | tf_op | source)
XLA Modules:
  0.0 114.8 jit_solution(18430763409458440988)
XLA Ops:
  0.6 1.4 %reshape.26 = f32[4,4,32,2,64]{4,3,2,1,0:T(2,128)S(1)} reshape(f32[4,4,4096]{2,1,0:T(4,128)} %param.19) | data formatting | bytes 524288 | tf_op jit(solution)/shard_map/reshape | solution.py:485
  2.0 0.3 copy.20
  2.4 0.0 copy-start
  2.4 1.0 reshape.27.trial
  3.4 0.0 copy-done
  3.4 0.1 reshape.24
  3.5 0.1 copy.17
  3.6 0.1 broadcast_in_dim.8
  3.8 0.0 copy-start.2
  3.8 1.0 reshape.25.pot
  4.8 0.0 copy-done.2
  4.8 0.6 reshape.22.sph
  6.1 106.7 %response.1 = (f32[1,4,2,768]{3,2,1,0:T(2,128)}, f32[4,4,128]{2,1,0:T(4,128)}) custom-call(s32[1,768]{1,0:T(1,128)} %reshape.22.sph, f32[16,2,768]{2,1,0:T(2,128)} %occ.1, f32[1,1]{1,0:T(1,128)} %bitcast.7.energy, f32[256,256]{1,0:T(8,128)} %reshape.25.pot, f32[256,256]{1,0:T(8,128)} %reshape.27.trial, bf16[128,64]{1,0:T(8,128)(2,1)} %constant.20.clone.zt_hi, ...), custom_call_target="tpu_custom_call" | custom-call | tf_op jit(solution)/shard_map/response/pallas_call | solution.py:520
  112.8 0.0 copy-start.1
  112.8 1.4 %copy.24 = f32[1,4,2,768]{3,2,1,0:T(2,128)} copy(f32[1,4,2,768]{3,2,1,0:T(2,128)} %get-tuple-element.4) | data formatting | bytes 49152
  114.2 0.0 copy-done.1
  114.2 0.6 copy.25
Async XLA Ops:
  2.4 1.0 copy-start
  3.8 1.0 copy-start.2
  112.8 1.4 %copy-start.1 = (f32[4,4,128]{2,1,0:T(4,128)S(1)}, f32[4,4,128]{2,1,0:T(4,128)}, u32[]{:S(2)}) copy-start(f32[4,4,128]{2,1,0:T(4,128)} %get-tuple-element.5) | copy-start | bytes 24580

commit v2 on v1

--- a/solution.py
+++ b/solution.py
@@ -57,10 +57,7 @@
                     x_tab[0, :, :, zl, k, cs, :, zl, ri] = value.real
                     x_tab[1, :, :, zl, k, cs, :, zl, ri] = value.imag
     x_tab = x_tab.reshape(512, 512)
-    tables = []
-    for table in (z_tab, y_tab, own_tab, x_tab, x_tab.T):
-        tables.extend(halves(table))
-    return tables
+    return list(halves(z_tab)) + [t.astype(np.float32) for t in (own_tab, x_tab, y_tab, x_tab.T, y_tab.T)]
 
 
 def split(value):
@@ -82,32 +79,54 @@
 
 
 def kernel(
-    sph, occ, energy, pot, trial,
-    zt_hi, zt_lo, y_hi, y_lo, o_hi, o_lo, t_hi, t_lo, tt_hi, tt_lo,
-    dpsi, dens,
+    sph, occ, energy, pot_in, trial_in, zt_hi, zt_lo, *refs,
+):
+    stored, (dpsi, dens), whole, kept, rest = refs[:5], refs[5:7], refs[7:12], refs[12:22], refs[22:]
+    o_hi, o_lo, t_hi, t_lo, y_hi, y_lo, tt_hi, tt_lo, yt_hi, yt_lo = kept
+    (
     gath, gath_hi, gath_lo, own, ztab_hi, ztab_lo, col_mask, rhs_hi, rhs_lo,
-    own_send, own_recv, send, recv, tile_send, tile_recv, full_send, full_recv, sum_send, sum_recv,
-    den_send, den_recv, own_field, field, ssem, rsem, gsend, grecv,
-):
+    own_send, own_recv, send, recv, pair_send, pair_recv, half_send, half_recv, full_recv, sum_send, sum_recv,
+    den_send, den_recv, own_field, field, pot, trial, ssem, rsem, gsend, grecv, tsem,
+    ) = rest
     g = lax.axis_index("grid")
     r = lax.axis_index("band")
     bx, bz = r // ZS, r % ZS
+    gy, gc = g // 2, g % 2
+
+    def ring(j, half):
+        return half + (1 - 2 * (j % 2)) * ((j + 1) // 2)
+
+    def grid_peer(k):
+        return 2 * ((gy + ring(k // 2, 4)) % 8) + (gc + k + 1) % 2
+
+    def band_peer(k):
+        return ZS * ((bx + ring(k % 4, 2)) % XS) + (bz + ring(k // 4, 4)) % ZS
 
     barrier = pltpu.get_barrier_semaphore()
 
     def greet_grid(k, carry):
-        pl.semaphore_signal(barrier, inc=1, device_id={"grid": (g + k) % GRID}, device_id_type=MESH)
+        pl.semaphore_signal(barrier, inc=1, device_id={"grid": grid_peer(k)}, device_id_type=MESH)
         return carry
 
     def greet_band(k, carry):
-        pl.semaphore_signal(barrier, inc=1, device_id={"band": (r + k) % BANDS}, device_id_type=MESH)
+        pl.semaphore_signal(barrier, inc=1, device_id={"band": band_peer(k)}, device_id_type=MESH)
         return carry
 
-    lax.fori_loop(1, GRID, greet_grid, 0)
-    lax.fori_loop(1, BANDS, greet_band, 0)
+    lax.fori_loop(0, BANDS - 1, greet_band, 0)
+    lax.fori_loop(0, GRID - 1, greet_grid, 0)
+
+    loads = [pltpu.make_async_copy(a, b, tsem.at[k]) for k, (a, b) in enumerate(zip(stored, whole))]
+    for load in loads:
+        load.start()
 
     def taken(ref, sem):
         pltpu.make_async_copy(ref, ref, sem).wait()
+
+    sent = []
+
+    def drain():
+        for ref, sem in sent:
+            taken(ref, sem)
 
     def to_band(src, dst, send_sem, recv_sem, x, z):
         pltpu.make_async_remote_copy(
@@ -115,7 +134,7 @@
             device_id={"band": x * ZS + z}, device_id_type=MESH,
         ).start()
 
-    place = sph[...]
+    place = sph[...].reshape(1, NJ)
     kz, xl, ky = place // 256, (place // 64) % 4, place % 64
     kx = g + 16 * xl
 
@@ -124,7 +143,7 @@
 
     fx, fy, fz = wave(kx), wave(ky), wave(kz)
     kinetic = KIN_SCALE * (fx * fx + fy * fy + fz * fz).astype(F32)
-    diag = jnp.concatenate([kinetic, kinetic], axis=1) - energy[0, 0]
+    diag = jnp.concatenate([kinetic, kinetic], axis=1) - energy[...].reshape(1, 1)
     one_z = jnp.where(lax.broadcasted_iota(jnp.int32, (32, NJ), 0) == (kz & 31), 1.0, 0.0).astype(BF16)
     column = (xl >> 1) * 32 + (ky & 31)
     one_col = jnp.where(lax.broadcasted_iota(jnp.int32, (64, NJ), 0) == column, 1.0, 0.0)
@@ -134,10 +153,34 @@
         lanes = pl.ds(ri * NJ, NJ)
         ztab_hi[:, lanes] = dot(zt_hi[:, 32 * ri : 32 * ri + 32], one_z, 1, 0).astype(BF16)
         ztab_lo[:, lanes] = dot(zt_lo[:, 32 * ri : 32 * ri + 32], one_z, 1, 0).astype(BF16)
+    left = lax.broadcasted_iota(jnp.int32, (4, 128), 1) < 64
+
+    def lay(t, carry):
+        lanes = pl.ds(pl.multiple_of(128 * t, 128), 128)
+        rows = pl.ds(pl.multiple_of(8 * t, 8), 8)
+        for q in range(3):
+            a, b = (pot_in[:, lanes],) * 2 if q == 2 else (trial_in[2 * q, :, lanes], trial_in[2 * q + 1, :, lanes])
+            even = jnp.where(left, a, pltpu.roll(b, 64, 1))
+            odd = jnp.where(left, pltpu.roll(a, 64, 1), b)
+            both = jnp.concatenate([even, odd], axis=0)
+            if q == 2:
+                pot[rows, :] = both
+            else:
+                trial[rows, 128 * q : 128 * q + 128] = both
+        return carry
+
+    lax.fori_loop(0, 32, lay, 0)
     own_z = pl.ds(pl.multiple_of(8 * bz, 8), 8)
     for part in range(2):
         for ri in range(2):
             gath[part, bx, own_z, NJ * ri : NJ * ri + NJ] = occ[8 * part : 8 * part + 8, ri, :]
+
+    for k, load in enumerate(loads):
+        load.wait()
+        for i in range(0, whole[k].shape[0], 64):
+            high, low = split(whole[k][i : i + 64, :])
+            kept[2 * k][i : i + 64, :] = high
+            kept[2 * k + 1][i : i + 64, :] = low
 
     pl.semaphore_wait(barrier, GRID - 1 + BANDS - 1)
 
@@ -156,6 +199,15 @@
 
         lax.fori_loop(jnp.where(r == 0, 1, 0), 16, give, 0)
 
+    def drain_own():
+        @pl.when(r == 0)
+        def _():
+            taken(occ.at[pl.ds(0, 15)], ssem.at[0])
+
+        @pl.when(r == 1)
+        def _():
+            taken(occ, ssem.at[0])
+
     def block(part, x, z):
         return gath.at[part, x, pl.ds(pl.multiple_of(8 * z, 8), 8)]
 
@@ -165,58 +217,69 @@
     z_up, z_dn = (bz + 1) % ZS, (bz + ZS - 1) % ZS
 
     def across(part, z, slot):
-        for k in range(1, XS):
+        for k in (2, 1, 3):
             to_band(block(part, bx, z), block(part, bx, z), gsend.at[slot], grecv.at[slot], (bx + k) % XS, bz)
+
+    def below(d):
+        return (bz + ZS - d) % ZS
+
+    def above(d):
+        return (bz + d) % ZS
+
+    def first(way, d, half):
+        return grecv.at[2 + 7 * way + (6 if d == 4 else 2 * d - 2 + half)]
+
+    def second(way, d):
+        return grecv.at[16 + 4 * way + d - 1]
+
+    def send_first(way, z, d, half):
+        ref = col(z, 2 * half, 2)
+        to_band(ref, ref, gsend.at[2], first(way, d, half), bx, z_dn if way else z_up)
+
+    def send_second(way, z, d):
+        to_band(block(1, bx, z), block(1, bx, z), gsend.at[3], second(way, d), bx, z_dn if way else z_up)
 
     def gather_0():
         across(0, bz, 0)
-        to_band(block(1, bx, bz), block(1, bx, bz), gsend.at[3], grecv.at[10], bx, z_up)
-        to_band(block(1, bx, bz), block(1, bx, bz), gsend.at[3], grecv.at[11], bx, z_dn)
+        for way in range(2):
+            send_second(way, bz, 1)
         across(1, bz, 1)
+        sent.append((gath.at[0, pl.ds(0, 3), pl.ds(0, 8)], gsend.at[0]))
+        sent.append((gath.at[1, pl.ds(0, 3)], gsend.at[1]))
+        sent.append((gath.at[0, :, pl.ds(0, 56)], gsend.at[2]))
+        sent.append((gath.at[0, 0, pl.ds(0, 56)], gsend.at[3]))
 
     def gather_1():
         taken(gath.at[0, pl.ds(0, 3), pl.ds(0, 8)], grecv.at[0])
-        to_band(col(bz), col(bz), gsend.at[2], grecv.at[2], bx, z_up)
-        to_band(col(bz), col(bz), gsend.at[2], grecv.at[3], bx, z_dn)
-        gather_part1(1)
-
-    def gather_part1(d):
-        below, above = (bz + ZS - d) % ZS, (bz + d) % ZS
-        taken(block(1, bx, below), grecv.at[8 + 2 * d])
-        to_band(block(1, bx, below), block(1, bx, below), gsend.at[3], grecv.at[10 + 2 * d], bx, z_up)
-        taken(block(1, bx, above), grecv.at[9 + 2 * d])
-        if d < 3:
-            to_band(block(1, bx, above), block(1, bx, above), gsend.at[3], grecv.at[11 + 2 * d], bx, z_dn)
-        across(1, below, 1)
-        across(1, above, 1)
-
-    def gather_mid(d):
-        below, above = (bz + ZS - d + 1) % ZS, (bz + d - 1) % ZS
-        taken(col(below), grecv.at[2 * d - 2])
-        to_band(col(below), col(below), gsend.at[2], grecv.at[2 * d], bx, z_up)
-        taken(col(above), grecv.at[2 * d - 1])
-        to_band(col(above), col(above), gsend.at[2], grecv.at[2 * d + 1], bx, z_dn)
-        gather_part1(d)
-
-    def gather_4():
-        below, above = (bz + ZS - 3) % ZS, (bz + 3) % ZS
-        taken(col(below), grecv.at[6])
-        to_band(col(below, 0, 2), col(below, 0, 2), gsend.at[2], grecv.at[8], bx, z_up)
-        taken(col(above), grecv.at[7])
-        to_band(col(above, 2, 2), col(above, 2, 2), gsend.at[2], grecv.at[9], bx, z_dn)
-        far = (bz + 4) % ZS
-        taken(block(1, bx, far), grecv.at[16])
-        across(1, far, 1)
-
-    def gather_5():
-        far = (bz + 4) % ZS
-        taken(col(far, 0, 2), grecv.at[8])
-        taken(col(far, 2, 2), grecv.at[9])
+        for half in range(2):
+            for way in range(2):
+                send_first(way, bz, 1, half)
+
+    def gather_first(d, half):
+        for way in range(2):
+            z = above(d) if way else below(d)
+            if d < 3 or half == way:
+                taken(col(z, 2 * half, 2), first(way, d, half))
+                send_first(way, z, d + 1, half)
+
+    def gather_second(d):
+        for way in range(1 if d == 4 else 2):
+            z = above(d) if way else below(d)
+            taken(block(1, bx, z), second(way, d))
+            if d + way < 4:
+                send_second(way, z, d + 1)
+            across(1, z, 1)
+
+    def gather_last():
+        taken(col(below(3), 2, 2), first(0, 3, 1))
+        taken(col(above(3), 0, 2), first(1, 3, 0))
+        taken(col(below(4), 0, 2), first(0, 4, 0))
+        taken(col(below(4), 2, 2), first(1, 4, 1))
         taken(gath.at[1, pl.ds(0, 3)], grecv.at[1])
 
     def exchange(src, dst, slot):
         def go(k, carry):
-            peer = (g + k) % GRID
+            peer = grid_peer(k)
             pltpu.make_async_remote_copy(
                 src_ref=src.at[pl.ds(pl.multiple_of(8 * peer, 8), 8)],
                 dst_ref=dst.at[pl.ds(pl.multiple_of(8 * g, 8), 8)],
@@ -225,43 +288,53 @@
             ).start()
             return carry
 
-        lax.fori_loop(1, GRID, go, 0)
+        lax.fori_loop(0, GRID - 1, go, 0)
+        sent.append((src.at[pl.ds(0, 8 * (GRID - 1))], ssem.at[slot]))
         here = pl.ds(pl.multiple_of(8 * g, 8), 8)
         dst[here, :] = src[here, :]
 
     def exchanged(dst, slot):
         taken(dst.at[pl.ds(0, 8 * (GRID - 1))], rsem.at[slot])
 
-    def tiles(n, slot):
+    other = 1 - gc
+
+    def to_other(src, dst, slot):
+        pltpu.make_async_remote_copy(
+            src_ref=src, dst_ref=dst, send_sem=ssem.at[slot], recv_sem=rsem.at[slot],
+            device_id={"grid": 2 * gy + other}, device_id_type=MESH,
+        ).start()
+        sent.append((src, ssem.at[slot]))
+
+    def across_chip(n, slot):
+        to_other(pair_send.at[n, pl.ds(2 * other, 2)], pair_recv.at[n], slot)
+
+    def across_ring(n, slot, slot_in):
+        taken(pair_recv.at[n], rsem.at[slot_in])
+        total = pair_send[n, pl.ds(2 * gc, 2)] + pair_recv[n]
+        half_send[n] = total
+
         def go(k, carry):
-            peer = (g + k) % GRID
             pltpu.make_async_remote_copy(
-                src_ref=tile_send.at[n, peer // 4], dst_ref=tile_recv.at[n, g],
+                src_ref=half_send.at[n], dst_ref=half_recv.at[n, gy],
                 send_sem=ssem.at[slot], recv_sem=rsem.at[slot],
-                device_id={"grid": peer}, device_id_type=MESH,
+                device_id={"grid": 2 * ((gy + ring(k, 4)) % 8) + gc}, device_id_type=MESH,
             ).start()
             return carry
 
-        lax.fori_loop(1, GRID, go, 0)
-        tile_recv[n, g] = tile_send[n, g // 4]
-
-    def tiles_sum(n, slot):
-        taken(tile_recv.at[n, pl.ds(0, GRID - 1)], rsem.at[slot])
-        return jnp.sum(tile_recv[n], axis=0)
+        lax.fori_loop(0, 7, go, 0)
+        sent.append((half_recv.at[n, pl.ds(0, 7)], ssem.at[slot]))
+        half_recv[n, gy] = total
+
+    def half_sum(n, slot):
+        taken(half_recv.at[n, pl.ds(0, 7)], rsem.at[slot])
+        return jnp.sum(half_recv[n], axis=0)
 
     def share(n, total, slot):
-        quarter = g // 4
-        full_send[n] = total
-        for k in range(1, 4):
-            pltpu.make_async_remote_copy(
-                src_ref=full_send.at[n], dst_ref=full_recv.at[n, quarter],
-                send_sem=ssem.at[slot], recv_sem=rsem.at[slot],
-                device_id={"grid": (g + 4 * k) % GRID}, device_id_type=MESH,
-            ).start()
-        full_recv[n, quarter] = total
+        full_recv[n, pl.ds(2 * gc, 2)] = total
+        to_other(full_recv.at[n, pl.ds(2 * gc, 2)], full_recv.at[n, pl.ds(2 * gc, 2)], slot)
 
     def shared(n, slot):
-        taken(full_recv.at[n, pl.ds(0, 3)], rsem.at[slot])
+        taken(full_recv.at[n, pl.ds(0, 2)], rsem.at[slot])
         return jnp.concatenate([full_recv[n, k] for k in range(4)], axis=1)
 
     def sums(n, value, slot):
@@ -271,11 +344,12 @@
             pltpu.make_async_remote_copy(
                 src_ref=sum_send.at[n], dst_ref=sum_recv.at[n, g],
                 send_sem=ssem.at[slot], recv_sem=rsem.at[slot],
-                device_id={"grid": (g + k) % GRID}, device_id_type=MESH,
+                device_id={"grid": grid_peer(k)}, device_id_type=MESH,
             ).start()
             return carry
 
-        lax.fori_loop(1, GRID, go, 0)
+        lax.fori_loop(0, GRID - 1, go, 0)
+        sent.append((sum_recv.at[n, pl.ds(0, GRID - 1)], ssem.at[slot]))
         sum_recv[n, g] = value
 
     def summed(n, slot):
@@ -304,7 +378,7 @@
         part = dot3(tt_hi[...], tt_lo[...], high, low)
         part = jnp.concatenate([part[128 * k : 128 * k + 128] for k in range(4)], axis=1)
         high, low = split(part)
-        return dot3(high, low, y_hi[...], y_lo[...], 1, 1)
+        return dot3(high, low, yt_hi[...], yt_lo[...])
 
     sub8 = lax.broadcasted_iota(jnp.int32, (8, 1), 0)
 
@@ -326,7 +400,7 @@
         second = dot(both, gath_lo[...], 1, 1)
         total = first[:8] + first[8:] + second[:8]
         for k in range(4):
-            tile_send[n, k] = total[:, 128 * k : 128 * k + 128]
+            pair_send[n, k] = total[:, 128 * k : 128 * k + 128]
 
     sign = jnp.where(sub8 < 4, 1.0, -1.0)
 
@@ -354,18 +428,25 @@
     own_send[...] = spread(jnp.concatenate([own_row, own_row], axis=0), 2)
     exchange(own_send, own_recv, 1)
     gather_1()
+    gather_second(1)
+    gather_first(1, 0)
+    gather_second(2)
+    gather_first(1, 1)
     exchanged(own_recv, 1)
     own_field[...] = to_planes(own_recv[...], o_hi, o_lo)
 
     weight = trial[...]
     send[0] = from_planes(jnp.concatenate([own_field[:256] * weight, own_field[256:] * weight], axis=0))
     exchange(send.at[0], recv.at[0], 2)
-    gather_mid(2)
-    gather_mid(3)
+    gather_first(2, 0)
+    gather_second(3)
+    gather_first(2, 1)
+    gather_second(4)
+    gather_first(3, 0)
+    gather_first(3, 1)
     exchanged(recv.at[0], 2)
     source = pick(recv[0])
-    gather_4()
-    gather_5()
+    gather_last()
 
     def round_pair(k, carry):
         rows = pl.ds(pl.multiple_of(16 * k, 16), 16)
@@ -376,22 +457,24 @@
 
     lax.fori_loop(0, 32, round_pair, 0)
     correlate(source, 0)
-    tiles(0, 3)
-    share(0, tiles_sum(0, 3), 4)
-    direction = expand(shared(0, 4)) - source
+    across_chip(0, 3)
+    across_ring(0, 4, 3)
+    share(0, half_sum(0, 4), 6)
+    direction = expand(shared(0, 6)) - source
 
     send[1] = spread(direction, PERTS)
     exchange(send.at[1], recv.at[1], 5)
     correlate(direction, 1)
-    tiles(1, 6)
+    across_chip(1, 8)
+    across_ring(1, 11, 8)
     exchanged(recv.at[1], 5)
     field[0] = to_planes(recv[1], y_hi, y_lo)
-    local = pot[...]
+    local = jnp.concatenate([pot[...], pot[...]], axis=1)
     send[2] = from_planes(jnp.concatenate([field[0, :256] * local, field[0, 256:] * local], axis=0))
     exchange(send.at[2], recv.at[2], 7)
-    corr_dir = tiles_sum(1, 6)
-    share(1, corr_dir, 8)
-    image = diag * direction + 2.0 * expand(shared(1, 8))
+    corr_dir = half_sum(1, 11)
+    share(1, corr_dir, 14)
+    image = diag * direction + 2.0 * expand(shared(1, 14))
     exchanged(recv.at[2], 7)
     image = image + pick(recv[2])
 
@@ -403,7 +486,8 @@
     dots = jnp.where(lane == 2, over_lanes(image * image), dots)
     sums(0, dots, 10)
     correlate(image, 2)
-    tiles(2, 11)
+    across_chip(2, 15)
+    across_ring(2, 16, 15)
     exchanged(recv.at[3], 9)
     field[1] = to_planes(recv[3], y_hi, y_lo)
     dots = summed(0, 10)
@@ -413,12 +497,12 @@
     grow = 1.0 + norm_next / norm
     direction1 = grow * direction - step0 * image
     field[1] = per_lane(grow) * field[0] - per_lane(step0) * field[1]
-    corr_dir1 = grow * corr_dir - step0 * tiles_sum(2, 11)
+    corr_dir1 = grow * corr_dir - step0 * half_sum(2, 16)
 
     energy_terms = over_lanes(diag * direction1 * direction1)
-    corr_terms = over_lanes(corr_dir1 * corr_dir1)
+    corr_terms = over_lanes(jnp.sum(corr_dir1 * corr_dir1, axis=0))
     corr_terms = corr_terms + pltpu.roll(jnp.broadcast_to(corr_terms, (8, 128)), 4, 0)[:, 0:1]
-    energy_terms = energy_terms + corr_terms * (2.0 / (2.0 * NPW) / 4.0)
+    energy_terms = energy_terms + corr_terms * (2.0 / (2.0 * NPW) / 8.0)
     real, imag = field[1, :256], field[1, 256:]
     squares = jnp.sum(local * (real * real + imag * imag), axis=0, keepdims=True)
     for p in range(PERTS):
@@ -433,7 +517,7 @@
     den_send[...] = dens0 + 2.0 * per_lane(step1) * dens1
 
     def give_density(k, carry):
-        peer = (r + k) % BANDS
+        peer = band_peer(k)
         pltpu.make_async_remote_copy(
             src_ref=den_send.at[pl.ds(pl.multiple_of(8 * peer, 8), 8)],
             dst_ref=den_recv.at[pl.ds(pl.multiple_of(8 * r, 8), 8)],
@@ -442,34 +526,16 @@
         ).start()
         return carry
 
-    lax.fori_loop(1, BANDS, give_density, 0)
+    lax.fori_loop(0, BANDS - 1, give_density, 0)
+    sent.append((den_send.at[pl.ds(0, 8 * (BANDS - 1))], ssem.at[13]))
     here = pl.ds(pl.multiple_of(8 * r, 8), 8)
     den_recv[here, :] = den_send[here, :]
     response = step0 * direction + step1 * direction1
     for ri in range(2):
         dpsi[0, :, ri, :] = response[:PERTS, NJ * ri : NJ * ri + NJ]
 
-    @pl.when(r == 0)
-    def _():
-        taken(occ.at[pl.ds(0, 15)], ssem.at[0])
-
-    @pl.when(r == 1)
-    def _():
-        taken(occ, ssem.at[0])
-
-    taken(own_send.at[pl.ds(0, 120)], ssem.at[1])
-    for n, slot in ((0, 2), (1, 5), (2, 7), (3, 9)):
-        taken(send.at[n, pl.ds(0, 120)], ssem.at[slot])
-    for n, slot in ((0, 3), (1, 6), (2, 11)):
-        taken(tile_recv.at[n, pl.ds(0, 15)], ssem.at[slot])
-    for n, slot in ((0, 4), (1, 8)):
-        taken(full_recv.at[n, pl.ds(0, 3)], ssem.at[slot])
-    for n, slot in ((0, 10), (1, 12)):
-        taken(sum_recv.at[n, pl.ds(0, 15)], ssem.at[slot])
-    taken(gath.at[0, pl.ds(0, 3), pl.ds(0, 8)], gsend.at[0])
-    taken(gath.at[1, pl.ds(0, 3)], gsend.at[1])
-    taken(gath.at[0, :, pl.ds(0, 56)], gsend.at[2])
-    taken(gath.at[0, 0, pl.ds(0, 56)], gsend.at[3])
+    drain()
+    drain_own()
 
     taken(den_recv.at[pl.ds(0, 8 * (BANDS - 1))], rsem.at[13])
     total = jnp.zeros((8, 256), F32)
@@ -478,17 +544,14 @@
     for p in range(PERTS):
         for half in range(2):
             dens[p, :, 64 * half : 64 * half + 64] = total[4 * half : 4 * half + 4, 64 * p : 64 * p + 64]
-    taken(den_send.at[pl.ds(0, 8 * (BANDS - 1))], ssem.at[13])
 
 
 def on_device(sphere_index, occupied, energies, local_pot, trial_pot):
-    trial = trial_pot.reshape(PERTS, 4, 32, 2, NG).transpose(2, 3, 1, 0, 4).reshape(256, 256)
-    pot = local_pot.reshape(4, 32, 2, 1, NG).transpose(1, 2, 0, 3, 4)
-    pot = jnp.broadcast_to(pot, (32, 2, 4, PERTS, NG)).reshape(256, 256)
     tables = [jnp.asarray(table) for table in make_tables()]
     vmem = pl.BlockSpec(memory_space=pltpu.VMEM)
-    smem = pl.BlockSpec(memory_space=pltpu.SMEM)
-    scratch = [
+    scratch = [pltpu.VMEM(table.shape, F32) for table in tables[2:]]
+    scratch += [pltpu.VMEM(table.shape, BF16) for table in tables[2:] for _ in range(2)]
+    scratch += [
         pltpu.VMEM((2, XS, 64, 2 * NJ), F32),
         pltpu.VMEM((512, 2 * NJ), BF16),
         pltpu.VMEM((512, 2 * NJ), BF16),
@@ -503,8 +566,9 @@
         pltpu.VMEM((4, 128, 256), F32),
         pltpu.VMEM((4, 128, 256), F32),
         pltpu.VMEM((3, 4, 8, 128), F32),
-        pltpu.VMEM((3, GRID, 8, 128), F32),
-        pltpu.VMEM((2, 8, 128), F32),
+        pltpu.VMEM((3, 2, 8, 128), F32),
+        pltpu.VMEM((3, 2, 8, 128), F32),
+        pltpu.VMEM((3, 8, 2, 8, 128), F32),
         pltpu.VMEM((2, 4, 8, 128), F32),
         pltpu.VMEM((2, 8, 128), F32),
         pltpu.VMEM((2, GRID, 8, 128), F32),
@@ -512,10 +576,13 @@
         pltpu.VMEM((256, 256), F32),
         pltpu.VMEM((512, 256), F32),
         pltpu.VMEM((2, 512, 256), F32),
-        pltpu.SemaphoreType.DMA((14,)),
-        pltpu.SemaphoreType.DMA((14,)),
+        pltpu.VMEM((256, 128), F32),
+        pltpu.VMEM((256, 256), F32),
+        pltpu.SemaphoreType.DMA((17,)),
+        pltpu.SemaphoreType.DMA((17,)),
         pltpu.SemaphoreType.DMA((4,)),
-        pltpu.SemaphoreType.DMA((17,)),
+        pltpu.SemaphoreType.DMA((23,)),
+        pltpu.SemaphoreType.DMA((5,)),
     ]
     return pl.pallas_call(
         kernel,
@@ -523,14 +590,14 @@
             jax.ShapeDtypeStruct((1, PERTS, 2, NJ), F32),
             jax.ShapeDtypeStruct((PERTS, 4, 128), F32),
         ),
-        in_specs=[vmem, vmem, smem] + [vmem] * 12,
+        in_specs=[vmem] * 7 + [pl.BlockSpec(memory_space=pl.ANY)] * 5,
         out_specs=(vmem, vmem),
         scratch_shapes=scratch,
         compiler_params=pltpu.CompilerParams(
-            collective_id=0, has_side_effects=True, vmem_limit_bytes=56 * 1024 * 1024
+            collective_id=0, has_side_effects=True, vmem_limit_bytes=60 * 1024 * 1024
         ),
         name="response",
-    )(sphere_index.reshape(1, NJ), occupied, energies.reshape(1, 1), pot, trial, *tables)
+    )(sphere_index, occupied, energies, local_pot, trial_pot, *tables)
 
 
 def solution(mesh):

time: 115 us -> 97.7 us (0.85)
  Pallas kernels: 107 us -> 94.3 us
  local copies, waits for them, and re-layouts: 6.69 us -> 1.96 us
    pallas_call x1, Pallas kernels: 107 us -> 94.3 us  [on_device(): pl.pallas_call(kernel, out_shape=(jax.ShapeDtypeStruct((1, PERTS, 2, NJ),...]
    reshape x6 -> x0, local copies, waits for them, and re-layouts: 4.5 us -> none  [the longest x3 2.75 us: on_device(): trial_pot.reshape(PERTS, 4, 32, 2, NG).transpose(2, 3, 1, 0, 4)]
where the time goes in v2:
time: 97.7 us; the launch traced here: 97.5 us
  Pallas kernels  94.3 us (97%)
  local copies, waits for them, and re-layouts  1.96 us (2%)
  between operations  1.29 us (1%)
    pallas_call x1, Pallas kernels, on_device(): pl.pallas_call(kernel, out_shape=(jax.ShapeDtypeStruct((1, PERTS, 2, NJ),...  94.3 us
    unnamed x4, local copies, waits for them, and re-layouts  1.96 us

profile of v2, /device:TPU:1, one launch (start us, length us, event | category | flops | bytes accessed | tf_op | source)
XLA Modules:
  0.0 97.5 jit_solution(10250795203287437315)
XLA Ops:
  1.3 94.3 %response.1 = (f32[1,4,2,768]{3,2,1,0:T(2,128)}, f32[4,4,128]{2,1,0:T(4,128)}) custom-call(s32[768]{0:T(1024)} %sph.1, f32[16,2,768]{2,1,0:T(2,128)} %occ.1, f32[1]{0:T(128)S(6)} %copy.16.energy, f32[4,4096]{1,0:T(4,128)} %pot_in.1, f32[4,4,4096]{2,1,0:T(4,128)} %trial_in.1, bf16[128,64]{1,0:T(8,128)(2,1)} %constant.14.clone.zt_hi, ...), custom_call_target="tpu_custom_call" | custom-call | tf_op jit(solution)/shard_map/response/pallas_call | solution.py:587
  95.6 0.0 copy-start
  95.6 1.4 %copy.17 = f32[1,4,2,768]{3,2,1,0:T(2,128)} copy(f32[1,4,2,768]{3,2,1,0:T(2,128)} %get-tuple-element.4) | data formatting | bytes 49152
  96.9 0.0 copy-done
  96.9 0.6 copy.18
Async XLA Ops:
  95.6 1.4 %copy-start = (f32[4,4,128]{2,1,0:T(4,128)S(1)}, f32[4,4,128]{2,1,0:T(4,128)}, u32[]{:S(2)}) copy-start(f32[4,4,128]{2,1,0:T(4,128)} %get-tuple-element.5) | copy-start | bytes 24580

commit v3 on v2

--- a/solution.py
+++ b/solution.py
@@ -13,6 +13,7 @@
 PERTS = 4
 GRID = 16
 XS, ZS = 4, 8
+CUT = 640
 BANDS = 32
 KIN_SCALE = 0.02
 MESH = pl.DeviceIdType.MESH
@@ -36,16 +37,16 @@
         value = phase * (1j**ri)
         z_tab[:, 0, ri], z_tab[:, 1, ri] = value.real, value.imag
     z_tab = z_tab.reshape(128, 64)
-    y_tab = np.zeros((PERTS, 2, 32, 2, 2, PERTS, NG))
-    own_tab = np.zeros((2, 2, 32, 2, 2, PERTS, NG))
-    for p in range(PERTS):
+    y_tab = np.zeros((2, 2, 32, 2, 2, 2, NG))
+    own_tab = np.zeros((2, 2, 32, 2, 2, 2, NG))
+    for p in range(2):
         for k in range(2):
             y_tab[p, k, :, k, 0, p] = phase.real.T
             y_tab[p, k, :, k, 1, p] = phase.imag.T
             own_tab[0, k, :, k, 0, p] = phase.real.T
             own_tab[0, k, :, k, 1, p] = phase.imag.T
-    y_tab = y_tab.reshape(256, 1024)
-    own_tab = own_tab.reshape(128, 1024)
+    y_tab = y_tab.reshape(128, 512)
+    own_tab = own_tab.reshape(128, 512)
     x_tab = np.zeros((2, 32, 2, 4, 2, 2, GRID, 4, 2))
     for k in range(2):
         rotor = np.exp(1j * angle * np.outer(np.arange(NG), np.arange(GRID) - 16 * k)) * norm
@@ -84,9 +85,9 @@
     stored, (dpsi, dens), whole, kept, rest = refs[:5], refs[5:7], refs[7:12], refs[12:22], refs[22:]
     o_hi, o_lo, t_hi, t_lo, y_hi, y_lo, tt_hi, tt_lo, yt_hi, yt_lo = kept
     (
-    gath, gath_hi, gath_lo, own, ztab_hi, ztab_lo, col_mask, rhs_hi, rhs_lo,
+    gath_x, gath_z, gath_hi, gath_lo, own, ztab_hi, ztab_lo, col_mask, rhs_hi, rhs_lo,
     own_send, own_recv, send, recv, pair_send, pair_recv, half_send, half_recv, full_recv, sum_send, sum_recv,
-    den_send, den_recv, own_field, field, pot, trial, ssem, rsem, gsend, grecv, tsem,
+    den_send, den_recv, coef_send, coef_recv, own_field, field, pot, trial, ssem, rsem, gsend, grecv, tsem,
     ) = rest
     g = lax.axis_index("grid")
     r = lax.axis_index("band")
@@ -170,10 +171,10 @@
         return carry
 
     lax.fori_loop(0, 32, lay, 0)
-    own_z = pl.ds(pl.multiple_of(8 * bz, 8), 8)
-    for part in range(2):
-        for ri in range(2):
-            gath[part, bx, own_z, NJ * ri : NJ * ri + NJ] = occ[8 * part : 8 * part + 8, ri, :]
+    mine = jnp.concatenate([occ[:, 0, :], occ[:, 1, :]], axis=1)
+    own_z = pl.ds(pl.multiple_of(16 * bz, 16), 16)
+    gath_x[bx, own_z, :] = mine[:, :CUT]
+    gath_z[bx, own_z, :] = mine[:, CUT:]
 
     for k, load in enumerate(loads):
         load.wait()
@@ -209,10 +210,10 @@
             taken(occ, ssem.at[0])
 
     def block(part, x, z):
-        return gath.at[part, x, pl.ds(pl.multiple_of(8 * z, 8), 8)]
+        return (gath_z if part else gath_x).at[x, pl.ds(pl.multiple_of(16 * z, 16), 16)]
 
     def col(z, first=0, count=XS):
-        return gath.at[0, pl.ds(first, count), pl.ds(pl.multiple_of(8 * z, 8), 8)]
+        return gath_x.at[pl.ds(first, count), pl.ds(pl.multiple_of(16 * z, 16), 16)]
 
     z_up, z_dn = (bz + 1) % ZS, (bz + ZS - 1) % ZS
 
@@ -244,13 +245,13 @@
         for way in range(2):
             send_second(way, bz, 1)
         across(1, bz, 1)
-        sent.append((gath.at[0, pl.ds(0, 3), pl.ds(0, 8)], gsend.at[0]))
-        sent.append((gath.at[1, pl.ds(0, 3)], gsend.at[1]))
-        sent.append((gath.at[0, :, pl.ds(0, 56)], gsend.at[2]))
-        sent.append((gath.at[0, 0, pl.ds(0, 56)], gsend.at[3]))
+        sent.append((gath_x.at[pl.ds(0, 3), pl.ds(0, 16)], gsend.at[0]))
+        sent.append((gath_z.at[pl.ds(0, 3)], gsend.at[1]))
+        sent.append((gath_x.at[:, pl.ds(0, 112)], gsend.at[2]))
+        sent.append((gath_z.at[0, pl.ds(0, 112)], gsend.at[3]))
 
     def gather_1():
-        taken(gath.at[0, pl.ds(0, 3), pl.ds(0, 8)], grecv.at[0])
+        taken(gath_x.at[pl.ds(0, 3), pl.ds(0, 16)], grecv.at[0])
         for half in range(2):
             for way in range(2):
                 send_first(way, bz, 1, half)
@@ -275,7 +276,7 @@
         taken(col(above(3), 0, 2), first(1, 3, 0))
         taken(col(below(4), 0, 2), first(0, 4, 0))
         taken(col(below(4), 2, 2), first(1, 4, 1))
-        taken(gath.at[1, pl.ds(0, 3)], grecv.at[1])
+        taken(gath_z.at[pl.ds(0, 3)], grecv.at[1])
 
     def exchange(src, dst, slot):
         def go(k, carry):
@@ -356,24 +357,23 @@
         taken(sum_recv.at[n, pl.ds(0, GRID - 1)], rsem.at[slot])
         return jnp.sum(sum_recv[n], axis=0)
 
-    def spread(rows, count):
-        for p in range(count):
-            row = rows[p : p + 1]
+    def spread(rows):
+        mask = col_mask[...]
+        for p, row in enumerate(rows):
             high = row.astype(BF16).astype(F32)
-            mask = col_mask[...]
             rhs_hi[64 * p : 64 * p + 64, :] = (mask * high).astype(BF16)
             rhs_lo[64 * p : 64 * p + 64, :] = (mask * (row - high)).astype(BF16)
-        wide = pl.ds(0, 64 * count)
-        return dot3(ztab_hi[...], ztab_lo[...], rhs_hi[wide, :], rhs_lo[wide, :], 1, 1)
+        return dot3(ztab_hi[...], ztab_lo[...], rhs_hi[...], rhs_lo[...], 1, 1)
 
     def to_planes(spectral, yh, yl):
         high, low = split(spectral)
         part = dot3(high, low, yh[...], yl[...])
-        part = jnp.concatenate([part[:, 256 * k : 256 * k + 256] for k in range(4)], axis=0)
+        part = jnp.concatenate([part[:, 128 * k : 128 * k + 128] for k in range(4)], axis=0)
         high, low = split(part)
         return dot3(t_hi[...], t_lo[...], high, low)
 
-    def from_planes(values):
+    def from_planes(values, factor):
+        values = jnp.concatenate([values[:256] * factor, values[256:] * factor], axis=0)
         high, low = split(values)
         part = dot3(tt_hi[...], tt_lo[...], high, low)
         part = jnp.concatenate([part[128 * k : 128 * k + 128] for k in range(4)], axis=1)
@@ -382,16 +382,28 @@
 
     sub8 = lax.broadcasted_iota(jnp.int32, (8, 1), 0)
 
-    def pick(spectral):
+    def pick(spectral, start, h):
         high, low = split(jnp.transpose(spectral))
-        result = jnp.zeros((8, 2 * NJ), F32)
-        for p in range(PERTS):
+        result = start
+        for p in range(2):
             rows = slice(64 * p, 64 * p + 64)
             box = dot3(high[rows], low[rows], ztab_hi[...], ztab_lo[...])
             line = jnp.sum(box * col_mask[...], axis=0, keepdims=True)
-            result = jnp.where(sub8 == p, line, result)
-            result = jnp.where(sub8 == p + 4, -turn(line), result)
+            result = result + jnp.where(sub8 == 2 * h + p, line, 0.0)
+            result = result + jnp.where(sub8 == 2 * h + p + 4, -turn(line), 0.0)
         return result
+
+    def forward(vector, n, h):
+        send[n, h] = spread([vector[2 * h + p : 2 * h + p + 1] for p in range(2)])
+        exchange(send.at[n, h], recv.at[n, h], 17 + 2 * n + h)
+
+    def arrived(n, h):
+        exchanged(recv.at[n, h], 17 + 2 * n + h)
+        return recv[n, h]
+
+    def backward(values, factor, n, h):
+        send[n, h] = from_planes(values, factor)
+        exchange(send.at[n, h], recv.at[n, h], 17 + 2 * n + h)
 
     def correlate(vector, n):
         high = vector.astype(BF16).astype(F32)
@@ -412,20 +424,49 @@
         direct = first[:8] + first[8:] + second[:8]
         return (direct + sign * turn(pltpu.roll(direct, 4, 0))) * (1.0 / (2.0 * NPW))
 
-    def per_lane(column_values):
-        which = lax.broadcasted_iota(jnp.int32, (1, 256), 1) // 64
-        result = jnp.zeros((1, 256), F32)
-        for p in range(PERTS):
-            result = jnp.where(which == p, column_values[p : p + 1, 0:1], result)
-        return result
+    lane = lax.broadcasted_iota(jnp.int32, (1, 128), 1)
+
+    def per_lane(column, h):
+        return jnp.where(lane < 64, column[2 * h : 2 * h + 1], column[2 * h + 1 : 2 * h + 2])
+
+    def as_row(columns):
+        total = jnp.zeros((8, 128), F32)
+        for k, column in enumerate(columns):
+            total = total + jnp.where(lane == sub8 + 8 * k, column, 0.0)
+        return jnp.sum(total, axis=0, keepdims=True)
+
+    def as_column(row, k):
+        return jnp.sum(jnp.where(lane == sub8 + 8 * k, row, 0.0), axis=1, keepdims=True)
 
     def over_lanes(value):
         return jnp.sum(value, axis=1, keepdims=True)
+
+    def to_all_bands(src, dst, slot, rows):
+        def go(k, carry):
+            peer = band_peer(k)
+            part = src if rows is None else src.at[pl.ds(pl.multiple_of(rows * peer, rows), rows)]
+            place = dst.at[r] if rows is None else dst.at[pl.ds(pl.multiple_of(rows * r, rows), rows)]
+            pltpu.make_async_remote_copy(
+                src_ref=part, dst_ref=place, send_sem=ssem.at[slot], recv_sem=rsem.at[slot],
+                device_id={"band": peer}, device_id_type=MESH,
+            ).start()
+            return carry
+
+        lax.fori_loop(0, BANDS - 1, go, 0)
+
+    def give_density(n, slot):
+        to_all_bands(den_send.at[n], den_recv.at[n], slot, 8)
+        sent.append((den_send.at[n, pl.ds(0, 8 * (BANDS - 1))], ssem.at[slot]))
+        here = pl.ds(pl.multiple_of(8 * r, 8), 8)
+        den_recv[n, here, :] = den_send[n, here, :]
+
+    def overlap(n, h, real, imag):
+        den_send[n, :, 128 * h : 128 * h + 128] = 2.0 * (own_field[:256] * real + own_field[256:] * imag)
 
     gather_0()
     taken(own, rsem.at[0])
     own_row = jnp.concatenate([own[0:1, :], own[1:2, :]], axis=1)
-    own_send[...] = spread(jnp.concatenate([own_row, own_row], axis=0), 2)
+    own_send[...] = spread([own_row, own_row])
     exchange(own_send, own_recv, 1)
     gather_1()
     gather_second(1)
@@ -435,24 +476,23 @@
     exchanged(own_recv, 1)
     own_field[...] = to_planes(own_recv[...], o_hi, o_lo)
 
-    weight = trial[...]
-    send[0] = from_planes(jnp.concatenate([own_field[:256] * weight, own_field[256:] * weight], axis=0))
-    exchange(send.at[0], recv.at[0], 2)
+    for h in range(2):
+        backward(own_field[...], trial[:, 128 * h : 128 * h + 128], 0, h)
     gather_first(2, 0)
     gather_second(3)
     gather_first(2, 1)
     gather_second(4)
     gather_first(3, 0)
     gather_first(3, 1)
-    exchanged(recv.at[0], 2)
-    source = pick(recv[0])
+    source = pick(arrived(0, 0), jnp.zeros((8, 2 * NJ), F32), 0)
+    source = pick(arrived(0, 1), source, 1)
     gather_last()
 
     def round_pair(k, carry):
         rows = pl.ds(pl.multiple_of(16 * k, 16), 16)
-        high, low = split(gath[k // 16, (k // 4) % 4, pl.ds(pl.multiple_of(16 * (k % 4), 16), 16), :])
-        gath_hi[rows, :] = high
-        gath_lo[rows, :] = low
+        from_rows = pl.ds(pl.multiple_of(16 * (k % ZS), 16), 16)
+        gath_hi[rows, :CUT], gath_lo[rows, :CUT] = split(gath_x[k // ZS, from_rows, :])
+        gath_hi[rows, CUT:], gath_lo[rows, CUT:] = split(gath_z[k // ZS, from_rows, :])
         return carry
 
     lax.fori_loop(0, 32, round_pair, 0)
@@ -462,74 +502,62 @@
     share(0, half_sum(0, 4), 6)
     direction = expand(shared(0, 6)) - source
 
-    send[1] = spread(direction, PERTS)
-    exchange(send.at[1], recv.at[1], 5)
+    for h in range(2):
+        forward(direction, 1, h)
     correlate(direction, 1)
     across_chip(1, 8)
     across_ring(1, 11, 8)
-    exchanged(recv.at[1], 5)
-    field[0] = to_planes(recv[1], y_hi, y_lo)
-    local = jnp.concatenate([pot[...], pot[...]], axis=1)
-    send[2] = from_planes(jnp.concatenate([field[0, :256] * local, field[0, 256:] * local], axis=0))
-    exchange(send.at[2], recv.at[2], 7)
+    local = pot[...]
+    for h in range(2):
+        field[0, h] = to_planes(arrived(1, h), y_hi, y_lo)
+        backward(field[0, h], local, 2, h)
     corr_dir = half_sum(1, 11)
     share(1, corr_dir, 14)
+    for h in range(2):
+        overlap(0, h, field[0, h, :256], field[0, h, 256:])
+    give_density(0, 13)
     image = diag * direction + 2.0 * expand(shared(1, 14))
-    exchanged(recv.at[2], 7)
-    image = image + pick(recv[2])
-
-    send[3] = spread(image, PERTS)
-    exchange(send.at[3], recv.at[3], 9)
-    lane = lax.broadcasted_iota(jnp.int32, (8, 128), 1)
-    dots = jnp.where(lane == 0, over_lanes(direction * direction), 0.0)
-    dots = jnp.where(lane == 1, over_lanes(direction * image), dots)
-    dots = jnp.where(lane == 2, over_lanes(image * image), dots)
-    sums(0, dots, 10)
+
+    for h in range(2):
+        image = pick(arrived(2, h), image, h)
+        forward(image, 3, h)
+    dots = [over_lanes(direction * direction), over_lanes(direction * image), over_lanes(image * image)]
+    sums(0, as_row(dots), 10)
     correlate(image, 2)
     across_chip(2, 15)
     across_ring(2, 16, 15)
-    exchanged(recv.at[3], 9)
-    field[1] = to_planes(recv[3], y_hi, y_lo)
+    for h in range(2):
+        field[1, h] = to_planes(arrived(3, h), y_hi, y_lo)
+        overlap(1, h, field[1, h, :256], field[1, h, 256:])
+    give_density(1, 9)
     dots = summed(0, 10)
-    norm = dots[:, 0:1]
-    step0 = norm / dots[:, 1:2]
-    norm_next = step0 * step0 * dots[:, 2:3] - norm
+    norm, curve, square = (as_column(dots, k) for k in range(3))
+    step0 = norm / curve
+    norm_next = step0 * step0 * square - norm
     grow = 1.0 + norm_next / norm
     direction1 = grow * direction - step0 * image
-    field[1] = per_lane(grow) * field[0] - per_lane(step0) * field[1]
     corr_dir1 = grow * corr_dir - step0 * half_sum(2, 16)
 
-    energy_terms = over_lanes(diag * direction1 * direction1)
+    terms = over_lanes(diag * direction1 * direction1)
     corr_terms = over_lanes(jnp.sum(corr_dir1 * corr_dir1, axis=0))
     corr_terms = corr_terms + pltpu.roll(jnp.broadcast_to(corr_terms, (8, 128)), 4, 0)[:, 0:1]
-    energy_terms = energy_terms + corr_terms * (2.0 / (2.0 * NPW) / 8.0)
-    real, imag = field[1, :256], field[1, 256:]
-    squares = jnp.sum(local * (real * real + imag * imag), axis=0, keepdims=True)
-    for p in range(PERTS):
-        piece = over_lanes(squares[:, 64 * p : 64 * p + 64])
-        energy_terms = energy_terms + jnp.where((sub8 % 4) == p, piece, 0.0)
-    sums(1, jnp.broadcast_to(energy_terms, (8, 128)), 12)
-    own_re, own_im = own_field[:256], own_field[256:]
-    dens0 = own_re * field[0, :256] + own_im * field[0, 256:]
-    dens1 = own_re * real + own_im * imag
-    dens0 = 2.0 * per_lane(step0) * dens0
-    step1 = norm_next / summed(1, 12)[:, 0:1]
-    den_send[...] = dens0 + 2.0 * per_lane(step1) * dens1
-
-    def give_density(k, carry):
-        peer = band_peer(k)
-        pltpu.make_async_remote_copy(
-            src_ref=den_send.at[pl.ds(pl.multiple_of(8 * peer, 8), 8)],
-            dst_ref=den_recv.at[pl.ds(pl.multiple_of(8 * r, 8), 8)],
-            send_sem=ssem.at[13], recv_sem=rsem.at[13],
-            device_id={"band": peer}, device_id_type=MESH,
-        ).start()
-        return carry
-
-    lax.fori_loop(0, BANDS - 1, give_density, 0)
-    sent.append((den_send.at[pl.ds(0, 8 * (BANDS - 1))], ssem.at[13]))
-    here = pl.ds(pl.multiple_of(8 * r, 8), 8)
-    den_recv[here, :] = den_send[here, :]
+    terms = terms + corr_terms * (2.0 / (2.0 * NPW) / 8.0)
+    for h in range(2):
+        mixed = per_lane(grow, h) * field[0, h] - per_lane(step0, h) * field[1, h]
+        real, imag = mixed[:256], mixed[256:]
+        squares = jnp.sum(local * (real * real + imag * imag), axis=0, keepdims=True)
+        for p in range(2):
+            piece = over_lanes(squares[:, 64 * p : 64 * p + 64])
+            terms = terms + jnp.where((sub8 % 4) == 2 * h + p, piece, 0.0)
+    sums(1, as_row([terms]), 12)
+    step1 = norm_next / as_column(summed(1, 12), 0)
+    weights = (step0 + step1 * grow, -(step1 * step0))
+    for n in range(2):
+        for h in range(2):
+            coef_send[2 * n + h : 2 * n + h + 1, :] = per_lane(weights[n], h)
+    to_all_bands(coef_send, coef_recv, 5, None)
+    sent.append((coef_recv.at[pl.ds(0, BANDS - 1)], ssem.at[5]))
+    coef_recv[r] = coef_send[...]
     response = step0 * direction + step1 * direction1
     for ri in range(2):
         dpsi[0, :, ri, :] = response[:PERTS, NJ * ri : NJ * ri + NJ]
@@ -537,13 +565,19 @@
     drain()
     drain_own()
 
-    taken(den_recv.at[pl.ds(0, 8 * (BANDS - 1))], rsem.at[13])
-    total = jnp.zeros((8, 256), F32)
-    for k in range(BANDS):
-        total = total + den_recv[8 * k : 8 * k + 8, :]
-    for p in range(PERTS):
-        for half in range(2):
-            dens[p, :, 64 * half : 64 * half + 64] = total[4 * half : 4 * half + 4, 64 * p : 64 * p + 64]
+    for n, slot in ((0, 13), (1, 9)):
+        taken(den_recv.at[n, pl.ds(0, 8 * (BANDS - 1))], rsem.at[slot])
+    taken(coef_recv.at[pl.ds(0, BANDS - 1)], rsem.at[5])
+    for h in range(2):
+        total = jnp.zeros((8, 128), F32)
+        for k in range(BANDS):
+            for n in range(2):
+                piece = den_recv[n, 8 * k : 8 * k + 8, 128 * h : 128 * h + 128]
+                total = total + coef_recv[k, 2 * n + h : 2 * n + h + 1, :] * piece
+        for p in range(2):
+            for half in range(2):
+                piece = total[4 * half : 4 * half + 4, 64 * p : 64 * p + 64]
+                dens[2 * h + p, :, 64 * half : 64 * half + 64] = piece
 
 
 def on_device(sphere_index, occupied, energies, local_pot, trial_pot):
@@ -552,34 +586,37 @@
     scratch = [pltpu.VMEM(table.shape, F32) for table in tables[2:]]
     scratch += [pltpu.VMEM(table.shape, BF16) for table in tables[2:] for _ in range(2)]
     scratch += [
-        pltpu.VMEM((2, XS, 64, 2 * NJ), F32),
+        pltpu.VMEM((XS, 128, CUT), F32),
+        pltpu.VMEM((XS, 128, 2 * NJ - CUT), F32),
         pltpu.VMEM((512, 2 * NJ), BF16),
         pltpu.VMEM((512, 2 * NJ), BF16),
         pltpu.VMEM((2, NJ), F32),
         pltpu.VMEM((128, 2 * NJ), BF16),
         pltpu.VMEM((128, 2 * NJ), BF16),
         pltpu.VMEM((64, 2 * NJ), F32),
-        pltpu.VMEM((256, 2 * NJ), BF16),
-        pltpu.VMEM((256, 2 * NJ), BF16),
+        pltpu.VMEM((128, 2 * NJ), BF16),
+        pltpu.VMEM((128, 2 * NJ), BF16),
         pltpu.VMEM((128, 128), F32),
         pltpu.VMEM((128, 128), F32),
-        pltpu.VMEM((4, 128, 256), F32),
-        pltpu.VMEM((4, 128, 256), F32),
+        pltpu.VMEM((4, 2, 128, 128), F32),
+        pltpu.VMEM((4, 2, 128, 128), F32),
         pltpu.VMEM((3, 4, 8, 128), F32),
         pltpu.VMEM((3, 2, 8, 128), F32),
         pltpu.VMEM((3, 2, 8, 128), F32),
         pltpu.VMEM((3, 8, 2, 8, 128), F32),
         pltpu.VMEM((2, 4, 8, 128), F32),
-        pltpu.VMEM((2, 8, 128), F32),
-        pltpu.VMEM((2, GRID, 8, 128), F32),
-        pltpu.VMEM((256, 256), F32),
-        pltpu.VMEM((256, 256), F32),
-        pltpu.VMEM((512, 256), F32),
-        pltpu.VMEM((2, 512, 256), F32),
+        pltpu.VMEM((2, 1, 128), F32),
+        pltpu.VMEM((2, GRID, 1, 128), F32),
+        pltpu.VMEM((2, 256, 256), F32),
+        pltpu.VMEM((2, 256, 256), F32),
+        pltpu.VMEM((4, 128), F32),
+        pltpu.VMEM((BANDS, 4, 128), F32),
+        pltpu.VMEM((512, 128), F32),
+        pltpu.VMEM((2, 2, 512, 128), F32),
         pltpu.VMEM((256, 128), F32),
         pltpu.VMEM((256, 256), F32),
-        pltpu.SemaphoreType.DMA((17,)),
-        pltpu.SemaphoreType.DMA((17,)),
+        pltpu.SemaphoreType.DMA((25,)),
+        pltpu.SemaphoreType.DMA((25,)),
         pltpu.SemaphoreType.DMA((4,)),
         pltpu.SemaphoreType.DMA((23,)),
         pltpu.SemaphoreType.DMA((5,)),

time: 97.7 us -> 93.1 us (0.953)
  Pallas kernels: 94.3 us -> 89.6 us
    pallas_call x1, Pallas kernels: 94.3 us -> 89.6 us  [on_device(): pl.pallas_call(kernel, out_shape=(jax.ShapeDtypeStruct((1, PERTS, 2, NJ),...]
where the time goes in v3:
time: 93.1 us; the launch traced here: 92.9 us
  Pallas kernels  89.6 us (96%)
  local copies, waits for them, and re-layouts  1.96 us (2%)
  between operations  1.29 us (1%)
    pallas_call x1, Pallas kernels, on_device(): pl.pallas_call(kernel, out_shape=(jax.ShapeDtypeStruct((1, PERTS, 2, NJ),...  89.6 us
    unnamed x4, local copies, waits for them, and re-layouts  1.96 us

profile of v3, /device:TPU:1, one launch (start us, length us, event | category | flops | bytes accessed | tf_op | source)
XLA Modules:
  0.0 92.9 jit_solution(16883488136564907785)
XLA Ops:
  1.3 89.6 %response.1 = (f32[1,4,2,768]{3,2,1,0:T(2,128)}, f32[4,4,128]{2,1,0:T(4,128)}) custom-call(s32[768]{0:T(1024)} %sph.1, f32[16,2,768]{2,1,0:T(2,128)} %occ.1, f32[1]{0:T(128)S(6)} %copy.16.energy, f32[4,4096]{1,0:T(4,128)} %pot_in.1, f32[4,4,4096]{2,1,0:T(4,128)} %trial_in.1, bf16[128,64]{1,0:T(8,128)(2,1)} %constant.14.clone.zt_hi, ...), custom_call_target="tpu_custom_call" | custom-call | tf_op jit(solution)/shard_map/response/pallas_call | solution.py:624
  90.9 0.0 copy-start
  90.9 1.4 %copy.17 = f32[1,4,2,768]{3,2,1,0:T(2,128)} copy(f32[1,4,2,768]{3,2,1,0:T(2,128)} %get-tuple-element.4) | data formatting | bytes 49152
  92.3 0.0 copy-done
  92.3 0.6 copy.18
Async XLA Ops:
  90.9 1.4 %copy-start = (f32[4,4,128]{2,1,0:T(4,128)S(1)}, f32[4,4,128]{2,1,0:T(4,128)}, u32[]{:S(2)}) copy-start(f32[4,4,128]{2,1,0:T(4,128)} %get-tuple-element.5) | copy-start | bytes 24580

commit v4 on v3

--- a/solution.py
+++ b/solution.py
@@ -80,14 +80,14 @@
 
 
 def kernel(
-    sph, occ, energy, pot_in, trial_in, zt_hi, zt_lo, *refs,
+    sph, occ_hbm, energy, pot_hbm, trial_hbm, zt_hi, zt_lo, *refs,
 ):
     stored, (dpsi, dens), whole, kept, rest = refs[:5], refs[5:7], refs[7:12], refs[12:22], refs[22:]
     o_hi, o_lo, t_hi, t_lo, y_hi, y_lo, tt_hi, tt_lo, yt_hi, yt_lo = kept
     (
     gath_x, gath_z, gath_hi, gath_lo, own, ztab_hi, ztab_lo, col_mask, rhs_hi, rhs_lo,
     own_send, own_recv, send, recv, pair_send, pair_recv, half_send, half_recv, full_recv, sum_send, sum_recv,
-    den_send, den_recv, coef_send, coef_recv, own_field, field, pot, trial, ssem, rsem, gsend, grecv, tsem,
+    den_send, den_recv, coef_send, coef_recv, own_field, field, pot, trial, occ, pot_in, trial_in, ssem, rsem, gsend, grecv, tsem,
     ) = rest
     g = lax.axis_index("grid")
     r = lax.axis_index("band")
@@ -117,7 +117,9 @@
     lax.fori_loop(0, GRID - 1, greet_grid, 0)
 
     loads = [pltpu.make_async_copy(a, b, tsem.at[k]) for k, (a, b) in enumerate(zip(stored, whole))]
-    for load in loads:
+    inputs = ((occ_hbm, occ), (pot_hbm, pot_in), (trial_hbm, trial_in))
+    inputs = [pltpu.make_async_copy(a, b, tsem.at[5 + k]) for k, (a, b) in enumerate(inputs)]
+    for load in inputs + loads:
         load.start()
 
     def taken(ref, sem):
@@ -154,6 +156,9 @@
         lanes = pl.ds(ri * NJ, NJ)
         ztab_hi[:, lanes] = dot(zt_hi[:, 32 * ri : 32 * ri + 32], one_z, 1, 0).astype(BF16)
         ztab_lo[:, lanes] = dot(zt_lo[:, 32 * ri : 32 * ri + 32], one_z, 1, 0).astype(BF16)
+    for load in inputs:
+        load.wait()
+
     left = lax.broadcasted_iota(jnp.int32, (4, 128), 1) < 64
 
     def lay(t, carry):
@@ -468,20 +473,20 @@
     own_row = jnp.concatenate([own[0:1, :], own[1:2, :]], axis=1)
     own_send[...] = spread([own_row, own_row])
     exchange(own_send, own_recv, 1)
+    gather_second(1)
     gather_1()
-    gather_second(1)
+    gather_second(2)
     gather_first(1, 0)
-    gather_second(2)
     gather_first(1, 1)
     exchanged(own_recv, 1)
     own_field[...] = to_planes(own_recv[...], o_hi, o_lo)
 
     for h in range(2):
         backward(own_field[...], trial[:, 128 * h : 128 * h + 128], 0, h)
+    gather_second(3)
     gather_first(2, 0)
-    gather_second(3)
+    gather_second(4)
     gather_first(2, 1)
-    gather_second(4)
     gather_first(3, 0)
     gather_first(3, 1)
     source = pick(arrived(0, 0), jnp.zeros((8, 2 * NJ), F32), 0)
@@ -562,9 +567,6 @@
     for ri in range(2):
         dpsi[0, :, ri, :] = response[:PERTS, NJ * ri : NJ * ri + NJ]
 
-    drain()
-    drain_own()
-
     for n, slot in ((0, 13), (1, 9)):
         taken(den_recv.at[n, pl.ds(0, 8 * (BANDS - 1))], rsem.at[slot])
     taken(coef_recv.at[pl.ds(0, BANDS - 1)], rsem.at[5])
@@ -579,10 +581,14 @@
                 piece = total[4 * half : 4 * half + 4, 64 * p : 64 * p + 64]
                 dens[2 * h + p, :, 64 * half : 64 * half + 64] = piece
 
+    drain()
+    drain_own()
+
 
 def on_device(sphere_index, occupied, energies, local_pot, trial_pot):
     tables = [jnp.asarray(table) for table in make_tables()]
     vmem = pl.BlockSpec(memory_space=pltpu.VMEM)
+    far = pl.BlockSpec(memory_space=pl.ANY)
     scratch = [pltpu.VMEM(table.shape, F32) for table in tables[2:]]
     scratch += [pltpu.VMEM(table.shape, BF16) for table in tables[2:] for _ in range(2)]
     scratch += [
@@ -615,11 +621,14 @@
         pltpu.VMEM((2, 2, 512, 128), F32),
         pltpu.VMEM((256, 128), F32),
         pltpu.VMEM((256, 256), F32),
+        pltpu.VMEM(occupied.shape, F32),
+        pltpu.VMEM(local_pot.shape, F32),
+        pltpu.VMEM(trial_pot.shape, F32),
         pltpu.SemaphoreType.DMA((25,)),
         pltpu.SemaphoreType.DMA((25,)),
         pltpu.SemaphoreType.DMA((4,)),
         pltpu.SemaphoreType.DMA((23,)),
-        pltpu.SemaphoreType.DMA((5,)),
+        pltpu.SemaphoreType.DMA((8,)),
     ]
     return pl.pallas_call(
         kernel,
@@ -627,7 +636,7 @@
             jax.ShapeDtypeStruct((1, PERTS, 2, NJ), F32),
             jax.ShapeDtypeStruct((PERTS, 4, 128), F32),
         ),
-        in_specs=[vmem] * 7 + [pl.BlockSpec(memory_space=pl.ANY)] * 5,
+        in_specs=[vmem, far, vmem, far, far, vmem, vmem] + [far] * 5,
         out_specs=(vmem, vmem),
         scratch_shapes=scratch,
         compiler_params=pltpu.CompilerParams(

time: 93.1 us -> 95 us (1.020)
  Pallas kernels: 89.6 us -> 91.5 us
    pallas_call x1, Pallas kernels: 89.6 us -> 91.5 us  [on_device(): pl.pallas_call(kernel, out_shape=(jax.ShapeDtypeStruct((1, PERTS, 2, NJ),...]
where the time goes in v4:
time: 95 us; the launch traced here: 94.7 us
  Pallas kernels  91.5 us (96%)
  local copies, waits for them, and re-layouts  1.96 us (2%)
  between operations  1.29 us (1%)
    pallas_call x1, Pallas kernels, on_device(): pl.pallas_call(kernel, out_shape=(jax.ShapeDtypeStruct((1, PERTS, 2, NJ),...  91.5 us
    unnamed x4, local copies, waits for them, and re-layouts  1.96 us

profile of v4, /device:TPU:1, one launch (start us, length us, event | category | flops | bytes accessed | tf_op | source)
XLA Modules:
  0.0 94.7 jit_solution(9926380859605552008)
XLA Ops:
  1.3 91.5 %response.1 = (f32[1,4,2,768]{3,2,1,0:T(2,128)}, f32[4,4,128]{2,1,0:T(4,128)}) custom-call(s32[768]{0:T(1024)} %sph.1, f32[16,2,768]{2,1,0:T(2,128)} %occ_hbm.1, f32[1]{0:T(128)S(6)} %copy.16.energy, f32[4,4096]{1,0:T(4,128)} %pot_hbm.1, f32[4,4,4096]{2,1,0:T(4,128)} %trial_hbm.1, bf16[128,64]{1,0:T(8,128)(2,1)} %constant.14.clone.zt_hi, ...), custom_call_target="tpu_custom_call" | custom-call | tf_op jit(solution)/shard_map/response/pallas_call | solution.py:633
  92.7 0.0 copy-start
  92.7 1.4 %copy.17 = f32[1,4,2,768]{3,2,1,0:T(2,128)} copy(f32[1,4,2,768]{3,2,1,0:T(2,128)} %get-tuple-element.4) | data formatting | bytes 49152
  94.1 0.0 copy-done
  94.1 0.6 copy.18
Async XLA Ops:
  92.7 1.4 %copy-start = (f32[4,4,128]{2,1,0:T(4,128)S(1)}, f32[4,4,128]{2,1,0:T(4,128)}, u32[]{:S(2)}) copy-start(f32[4,4,128]{2,1,0:T(4,128)} %get-tuple-element.5) | copy-start | bytes 24580

commit v5 on v4

--- a/solution.py
+++ b/solution.py
@@ -473,20 +473,20 @@
     own_row = jnp.concatenate([own[0:1, :], own[1:2, :]], axis=1)
     own_send[...] = spread([own_row, own_row])
     exchange(own_send, own_recv, 1)
+    gather_1()
     gather_second(1)
-    gather_1()
+    gather_first(1, 0)
     gather_second(2)
-    gather_first(1, 0)
     gather_first(1, 1)
     exchanged(own_recv, 1)
     own_field[...] = to_planes(own_recv[...], o_hi, o_lo)
 
     for h in range(2):
         backward(own_field[...], trial[:, 128 * h : 128 * h + 128], 0, h)
+    gather_first(2, 0)
     gather_second(3)
-    gather_first(2, 0)
+    gather_first(2, 1)
     gather_second(4)
-    gather_first(2, 1)
     gather_first(3, 0)
     gather_first(3, 1)
     source = pick(arrived(0, 0), jnp.zeros((8, 2 * NJ), F32), 0)
@@ -561,11 +561,13 @@
         for h in range(2):
             coef_send[2 * n + h : 2 * n + h + 1, :] = per_lane(weights[n], h)
     to_all_bands(coef_send, coef_recv, 5, None)
-    sent.append((coef_recv.at[pl.ds(0, BANDS - 1)], ssem.at[5]))
     coef_recv[r] = coef_send[...]
     response = step0 * direction + step1 * direction1
     for ri in range(2):
         dpsi[0, :, ri, :] = response[:PERTS, NJ * ri : NJ * ri + NJ]
+
+    drain()
+    drain_own()
 
     for n, slot in ((0, 13), (1, 9)):
         taken(den_recv.at[n, pl.ds(0, 8 * (BANDS - 1))], rsem.at[slot])
@@ -581,8 +583,7 @@
                 piece = total[4 * half : 4 * half + 4, 64 * p : 64 * p + 64]
                 dens[2 * h + p, :, 64 * half : 64 * half + 64] = piece
 
-    drain()
-    drain_own()
+    taken(coef_recv.at[pl.ds(0, BANDS - 1)], ssem.at[5])
 
 
 def on_device(sphere_index, occupied, energies, local_pot, trial_pot):

time: 95 us -> 93 us (0.979)
  Pallas kernels: 91.5 us -> 89.5 us
    pallas_call x1, Pallas kernels: 91.5 us -> 89.5 us  [on_device(): pl.pallas_call(kernel, out_shape=(jax.ShapeDtypeStruct((1, PERTS, 2, NJ),...]
where the time goes in v5:
time: 93 us; the launch traced here: 92.7 us
  Pallas kernels  89.5 us (96%)
  local copies, waits for them, and re-layouts  1.96 us (2%)
  between operations  1.29 us (1%)
    pallas_call x1, Pallas kernels, on_device(): pl.pallas_call(kernel, out_shape=(jax.ShapeDtypeStruct((1, PERTS, 2, NJ),...  89.5 us
    unnamed x4, local copies, waits for them, and re-layouts  1.96 us

profile of v5, /device:TPU:1, one launch (start us, length us, event | category | flops | bytes accessed | tf_op | source)
XLA Modules:
  0.0 92.7 jit_solution(13942609246622974495)
XLA Ops:
  1.3 89.5 %response.1 = (f32[1,4,2,768]{3,2,1,0:T(2,128)}, f32[4,4,128]{2,1,0:T(4,128)}) custom-call(s32[768]{0:T(1024)} %sph.1, f32[16,2,768]{2,1,0:T(2,128)} %occ_hbm.1, f32[1]{0:T(128)S(6)} %copy.16.energy, f32[4,4096]{1,0:T(4,128)} %pot_hbm.1, f32[4,4,4096]{2,1,0:T(4,128)} %trial_hbm.1, bf16[128,64]{1,0:T(8,128)(2,1)} %constant.14.clone.zt_hi, ...), custom_call_target="tpu_custom_call" | custom-call | tf_op jit(solution)/shard_map/response/pallas_call | solution.py:634
  90.8 0.0 copy-start
  90.8 1.4 %copy.17 = f32[1,4,2,768]{3,2,1,0:T(2,128)} copy(f32[1,4,2,768]{3,2,1,0:T(2,128)} %get-tuple-element.4) | data formatting | bytes 49152
  92.1 0.0 copy-done
  92.1 0.6 copy.18
Async XLA Ops:
  90.8 1.4 %copy-start = (f32[4,4,128]{2,1,0:T(4,128)S(1)}, f32[4,4,128]{2,1,0:T(4,128)}, u32[]{:S(2)}) copy-start(f32[4,4,128]{2,1,0:T(4,128)} %get-tuple-element.5) | copy-start | bytes 24580
